TPU v7x, 32 devices: a whole 2x2x4 slice. The times are simulated.
32 devices in a mesh: curve: 8 (over z, x), tile: 4 (over y, core).
Axes of the slice: x: 2, y: 2, z: 4, core: 2. Of those that a mesh axis runs over, the one named last changes fastest.
Arguments:
- state: float32 [5, 1024, 512], P(None, ('curve', 'tile')), may hold values from -6 to 6
- levels: int32 [1024], P(('curve', 'tile')), may hold values from 0 to 2
- send_faces: int32 [128, 4], P(('curve', 'tile')), may hold values from 0 to 959, as said below
- send_counts: int32 [128], P(('curve', 'tile')), may hold values from 0 to 4, as said below
- recv_faces: int32 [128, 4], P(('curve', 'tile')), may hold values from 0 to 191, as said below
- recv_orients: int32 [128, 4], P(('curve', 'tile')), may hold values from 0 to 7, as said below
- recv_counts: int32 [128], P(('curve', 'tile')), may hold values from 0 to 4
- curve_faces: int32 [64, 16], P(('curve', 'tile')), may hold values from 0 to 191, as said below
- curve_orients: int32 [64, 16], P(('curve', 'tile')), may hold values from 0 to 7, as said below
- curve_counts: int32 [64], P(('curve', 'tile')), may hold values from 0 to 16, as said below
Outputs:
- advanced: float32 [5, 1024, 512], P(None, ('curve', 'tile'))
Inputs may be any that keep to these rules, and one draw needn't show every extreme that they name: `send_faces`: row p of device (b, t) lists in its first send_counts entries the pairs it shares with device (b, p): (6 e + f) 5 + c with f 3 or 5 and c 0 to 3 for a half-face mortar of a coarse face, 4 for a whole face; each coarse face listed has its four children 0 to 3 listed once each, possibly with different peers; any other face id appears at most once in all lists of a device; entries past the count are 0. `send_counts`: the count of device (b, t) for peer p equals the receive count of device (b, p) for peer t. `recv_faces`: slot k of row t of device (b, p) is face 6 e + f paired with slot k of row p of device (b, t), with f = 2 where the sender's face is 3 and 4 where it is 5; entries past the count are 0. `recv_orients`: R_o maps the sender's node order into the receiver's; 0 past the count. `curve_faces`: row 0 names faces with f = 0, row 1 faces with f = 1; slot k of row 1 of device (b, t) pairs with slot k of row 0 of device (b + 1, t); entries past the count are 0. `curve_orients`: the two sides of a pair hold mutually inverse orientations; 0 past the count. `curve_counts`: both sides of a pair of rows hold the same count; it is 0 towards a curve index that does not exist.
All inputs are finite; a program needn't handle non-finite values.
Results may differ from a plain program's by a relative error of at most 0.0003.
Values sent between devices are 32-bit elements; how exact they have to be, the bound alone decides.
A program may use at most 64 MiB of HBM per device.

v0:
```python
import jax
import jax.numpy as jnp
import numpy as np
from jax import lax
from jax.sharding import PartitionSpec as P

time_step = 0.002
wave_speed = 1.0
highest = lax.Precision.HIGHEST
inner_nodes = [
    -0.8717401485096066,
    -0.5917001814331423,
    -0.20929921790247888,
    0.20929921790247888,
    0.5917001814331423,
    0.8717401485096066,
]


def with_halo(block, sides, width):
    for axis, dim in sides:
        count = lax.axis_size(axis)
        forward = [(i, i + 1) for i in range(count - 1)]
        backward = [(target, source) for source, target in forward]
        low = lax.ppermute(
            lax.slice_in_dim(block, block.shape[dim] - width, None, axis=dim), axis, forward
        )
        high = lax.ppermute(lax.slice_in_dim(block, 0, width, axis=dim), axis, backward)
        block = jnp.concatenate([low, block, high], axis=dim)
    return block


def legendre_seven(abscissa):
    before = abscissa * 0.0 + 1.0
    current = abscissa + 0.0
    for order in range(1, 7):
        before, current = (
            current,
            ((2 * order + 1) * abscissa * current - order * before) / (order + 1),
        )
    return current


def basis_tables():
    degree = 7
    points = np.array([-1.0] + inner_nodes + [1.0])
    values = legendre_seven(points)
    weights = 2.0 / (degree * (degree + 1) * values**2)
    deriv_mat = np.zeros((8, 8))
    for row_at in range(8):
        for col_at in range(8):
            if row_at != col_at:
                deriv_mat[row_at, col_at] = values[row_at] / (
                    values[col_at] * (points[row_at] - points[col_at])
                )
    deriv_mat[0, 0] = -degree * (degree + 1) / 4.0
    deriv_mat[7, 7] = degree * (degree + 1) / 4.0
    halves = []
    projections = []
    for half_side in range(2):
        targets = (points + 2.0 * half_side - 1.0) / 2.0
        interp = np.ones((8, 8))
        for col_at in range(8):
            for other_at in range(8):
                if other_at != col_at:
                    interp[:, col_at] *= (targets - points[other_at]) / (
                        points[col_at] - points[other_at]
                    )
        halves.append(interp)
        projections.append(0.5 * (interp.T * weights[None, :]) / weights[:, None])
    interp_mats = np.stack(
        [
            np.kron(halves[first_at], halves[second_at])
            for first_at in range(2)
            for second_at in range(2)
        ]
        + [np.eye(64)]
    )
    proj_mats = np.stack(
        [
            np.kron(projections[first_at], projections[second_at])
            for first_at in range(2)
            for second_at in range(2)
        ]
        + [np.eye(64)]
    )
    perm_table = np.zeros((8, 64), np.int32)
    for orient_code in range(8):
        for first_at in range(8):
            for second_at in range(8):
                if orient_code & 4:
                    upper_at, lower_at = (second_at, first_at)
                else:
                    upper_at, lower_at = (first_at, second_at)
                if orient_code & 1:
                    upper_at = 7 - upper_at
                if orient_code & 2:
                    lower_at = 7 - lower_at
                perm_table[orient_code, 8 * first_at + second_at] = 8 * upper_at + lower_at
    inverse_table = np.argsort(perm_table, axis=1).astype(np.int32)
    deriv_first = np.kron(deriv_mat, np.eye(64))
    deriv_second = np.kron(np.eye(8), np.kron(deriv_mat, np.eye(8)))
    deriv_third = np.kron(np.eye(64), deriv_mat)
    selector = np.zeros((512, 384))
    for first_at in range(8):
        for second_at in range(8):
            column = 8 * first_at + second_at
            for side_at in range(2):
                edge = 7 * side_at
                selector[64 * edge + 8 * first_at + second_at, 64 * side_at + column] = 1.0
                selector[64 * first_at + 8 * edge + second_at, 64 * (2 + side_at) + column] = 1.0
                selector[64 * first_at + 8 * second_at + edge, 64 * (4 + side_at) + column] = 1.0
    lift_end = float(1.0 / weights[0])
    return (
        jnp.asarray(interp_mats, jnp.float32),
        jnp.asarray(proj_mats, jnp.float32),
        jnp.asarray(perm_table, jnp.int32),
        jnp.asarray(inverse_table, jnp.int32),
        lift_end,
        jnp.asarray(deriv_first, jnp.float32),
        jnp.asarray(deriv_second, jnp.float32),
        jnp.asarray(deriv_third, jnp.float32),
        jnp.asarray(selector, jnp.float32),
    )


def face_traces(current, selector):
    fields, elements, npoints = current.shape
    flat = jnp.dot(current.reshape(fields * elements, npoints), selector, precision=highest)
    return flat.reshape(fields, elements * 6, 64)


def spread_faces(jump_term, elements, selector):
    fields = jump_term.shape[0]
    flat = jnp.dot(jump_term.reshape(fields * elements, 384), selector.T, precision=highest)
    return flat.reshape(fields, elements, 512)


def dim_picks(face_ids):
    return ((face_ids % 6 // 2)[None, :] == jnp.arange(3, dtype=jnp.int32)[:, None]).astype(
        jnp.float32
    )


def normal_flux(trace_set, face_ids):
    pick_mask = dim_picks(face_ids)
    sign_vals = (face_ids % 2 * 2 - 1).astype(jnp.float32)[:, None]
    normal_vel = jnp.sum(pick_mask[:, :, None] * trace_set[1:4], axis=0)
    pressure = sign_vals * trace_set[4]
    return jnp.stack(
        [
            sign_vals * normal_vel,
            pick_mask[0][:, None] * pressure,
            pick_mask[1][:, None] * pressure,
            pick_mask[2][:, None] * pressure,
            sign_vals * normal_vel,
        ]
    )


def wall_state(own_side, face_ids):
    flip_vals = 1.0 - 2.0 * dim_picks(face_ids)
    return jnp.concatenate(
        [own_side[:1], own_side[1:4] * flip_vals[:, :, None], own_side[4:]], axis=0
    )


def rusanov(own_side, other_side, face_ids):
    average = 0.5 * (normal_flux(own_side, face_ids) + normal_flux(other_side, face_ids))
    return average - 0.5 * wave_speed * (other_side - own_side)


def orient(values, orient_codes, lookup):
    matches = (orient_codes[:, None] == jnp.arange(8, dtype=jnp.int32)[None, :]).astype(jnp.int32)
    gather_index = jnp.sum(matches[:, :, None] * lookup[None, :, :], axis=1)
    return jnp.take_along_axis(values, jnp.broadcast_to(gather_index[None], values.shape), axis=2)


def child_apply(values, child_ids, matrices):
    mapped = jnp.einsum("fnj,cij->cfni", values, matrices, precision=highest)
    pick_mask = (child_ids[None, :] == jnp.arange(5, dtype=jnp.int32)[:, None]).astype(jnp.float32)
    return jnp.sum(pick_mask[:, None, :, None] * mapped, axis=0)


def volume_term(current, deriv_first, deriv_second, deriv_third):
    fields, elements, npoints = current.shape
    grad_x = jnp.dot(
        current[1:5:3].reshape(2 * elements, 512), deriv_first.T, precision=highest
    ).reshape(2, elements, 512)
    grad_y = jnp.dot(
        current[2:5:2].reshape(2 * elements, 512), deriv_second.T, precision=highest
    ).reshape(2, elements, 512)
    grad_z = jnp.dot(
        current[3:5].reshape(2 * elements, 512), deriv_third.T, precision=highest
    ).reshape(2, elements, 512)
    diverge = grad_x[0] + grad_y[0] + grad_z[0]
    return -jnp.stack([diverge, grad_x[1], grad_y[1], grad_z[1], diverge])


def shards(
    state,
    levels,
    send_faces,
    send_counts,
    recv_faces,
    recv_orients,
    recv_counts,
    curve_faces,
    curve_orients,
    curve_counts,
):
    (
        interp_mats,
        proj_mats,
        perm_table,
        inverse_table,
        lift_end,
        deriv_first,
        deriv_second,
        deriv_third,
        selector,
    ) = basis_tables()
    fields, elements, npoints = state.shape
    face_total = elements * 6
    tile_total, slot_total = send_faces.shape
    rim_slots = curve_faces.shape[1]
    block_width = slot_total * 64
    scales = jnp.exp2(levels.astype(jnp.float32))
    face_scales = jnp.repeat(scales, 6) * lift_end
    slot_range = jnp.arange(slot_total, dtype=jnp.int32)
    send_live = slot_range[None, :] < send_counts[:, None]
    send_ids = jnp.where(send_live, send_faces // 5, face_total).reshape(-1)
    child_ids = (send_faces % 5).reshape(-1)
    send_mask = send_live.reshape(-1).astype(jnp.float32)[None, :, None]
    recv_live = slot_range[None, :] < recv_counts[:, None]
    recv_ids = jnp.where(recv_live, recv_faces, face_total).reshape(-1)
    recv_codes = recv_orients.reshape(-1)
    recv_mask = recv_live.reshape(-1).astype(jnp.float32)[None, :, None]
    curve_live = jnp.arange(rim_slots, dtype=jnp.int32)[None, :] < curve_counts[:, None]
    curve_ids = jnp.where(curve_live, curve_faces, face_total).reshape(-1)
    curve_codes = curve_orients.reshape(-1)
    curve_mask = curve_live.reshape(-1).astype(jnp.float32)[None, :, None]
    all_faces = jnp.arange(face_total, dtype=jnp.int32)

    def rhs(current):
        traces = face_traces(current, selector)
        padded = jnp.concatenate([traces, jnp.zeros((fields, 1, 64), jnp.float32)], axis=1)
        mortar = child_apply(padded[:, send_ids], child_ids, interp_mats) * send_mask
        own_recv = padded[:, recv_ids]
        own_curve = padded[:, curve_ids]
        fine_home = orient(own_recv, recv_codes, inverse_table) * recv_mask
        outgoing = jnp.concatenate(
            [
                mortar.reshape(fields, tile_total, block_width),
                fine_home.reshape(fields, tile_total, block_width),
            ],
            axis=2,
        )
        arrived = lax.all_to_all(outgoing, "tile", split_axis=1, concat_axis=1, tiled=True)
        coarse_in = arrived[:, :, :block_width].reshape(fields, -1, 64)
        fine_in = arrived[:, :, block_width:].reshape(fields, -1, 64)
        fine_flux = (
            rusanov(own_recv, orient(coarse_in, recv_codes, perm_table), recv_ids) * recv_mask
        )
        coarse_flux = rusanov(mortar, fine_in, send_ids) * send_mask
        extended = with_halo(own_curve.reshape(fields, 2, rim_slots * 64), (("curve", 1),), 1)
        neighbours = jnp.concatenate([extended[:, 0], extended[:, 3]], axis=1).reshape(
            fields, 2 * rim_slots, 64
        )
        curve_flux = (
            rusanov(own_curve, orient(neighbours, curve_codes, perm_table), curve_ids) * curve_mask
        )
        accumulated = jnp.zeros((fields, face_total + 1, 64), jnp.float32)
        accumulated = accumulated.at[:, send_ids].add(
            child_apply(coarse_flux, child_ids, proj_mats)
        )
        accumulated = accumulated.at[:, recv_ids].add(fine_flux)
        accumulated = accumulated.at[:, curve_ids].add(curve_flux)
        listed = jnp.zeros((face_total + 1,), jnp.float32)
        listed = listed.at[send_ids].add(1.0).at[recv_ids].add(1.0).at[curve_ids].add(1.0)
        wall_flux = rusanov(traces, wall_state(traces, all_faces), all_faces)
        flux_star = jnp.where(
            listed[None, :face_total, None] > 0.0, accumulated[:, :face_total], wall_flux
        )
        jump_term = (normal_flux(traces, all_faces) - flux_star) * face_scales[None, :, None]
        volume = volume_term(current, deriv_first, deriv_second, deriv_third)
        return volume * scales[None, :, None] + spread_faces(jump_term, elements, selector)

    section_one = state + time_step * rhs(state)
    section_two = 0.75 * state + 0.25 * (section_one + time_step * rhs(section_one))
    return state / 3.0 + 2.0 / 3.0 * (section_two + time_step * rhs(section_two))


def solution(mesh):
    return jax.shard_map(
        shards,
        mesh=mesh,
        in_specs=(
            P(None, ("curve", "tile"), None),
            P(("curve", "tile")),
            P(("curve", "tile"), None),
            P(("curve", "tile")),
            P(("curve", "tile"), None),
            P(("curve", "tile"), None),
            P(("curve", "tile")),
            P(("curve", "tile"), None),
            P(("curve", "tile"), None),
            P(("curve", "tile")),
        ),
        out_specs=P(None, ("curve", "tile"), None),
        check_vma=False,
    )
```

profile of v0, /device:TPU:0, one launch (start us, length us, event | category | flops | bytes accessed | tf_op | source)
XLA Modules:
  0.0 759.9 jit_solution(12439333879142372713)
XLA Ops:
  6.0 5.4 collective-permute-start
  14.5 42.8 %gather_fusion.9 = f32[5120]{0:T(1024)S(1)} fusion(f32[5,16,64]{2,1,0:T(8,128)S(1)} %bitcast.362, s32[5120]{0:T(1024)S(1)} %reshape.3220), kind=kCustom, calls=%fused_computation.clone | custom fusion | bytes 102400 | tf_op jit(solution)/shard_map/jit(take_along_axis)/gather | solution.py:176
  60.1 3.9 all-to-all-start
  97.3 85.2 %gather_fusion.11 = f32[10240]{0:T(1024)S(1)} fusion(f32[5,32,64]{2,1,0:T(8,128)S(1)} %pad_maximum_fusion, s32[10240]{0:T(1024)S(1)} %reshape.3230), kind=kCustom, calls=%fused_computation.1.clone | custom fusion | bytes 204800 | tf_op jit(solution)/shard_map/jit(take_along_axis)/gather | solution.py:176
  193.1 42.8 %gather_fusion.10 = f32[5120]{0:T(1024)S(1)} fusion(f32[5,16,64]{2,1,0:T(8,128)S(1)} %reshape.2921, s32[5120]{0:T(1024)S(1)} %reshape.3225), kind=kCustom, calls=%fused_computation.2.clone | custom fusion | bytes 102400 | tf_op jit(solution)/shard_map/jit(take_along_axis)/gather | solution.py:176
  250.2 2.6 scatter_fusion.2
  252.8 2.6 scatter_fusion.3
  255.4 4.4 scatter_fusion.4
  277.2 2.5 gather_fusion.5
  296.0 4.5 collective-permute-start.2
  301.9 42.8 %gather_fusion.12 = f32[5120]{0:T(1024)S(1)} fusion(f32[5,16,64]{2,1,0:T(8,128)S(1)} %bitcast.372, s32[5120]{0:T(1024)S(1)} %reshape.3220), kind=kCustom, calls=%fused_computation.3.clone | custom fusion | bytes 102400 | tf_op jit(solution)/shard_map/jit(take_along_axis)/gather | solution.py:176
  349.1 4.1 all-to-all-start.1
  365.7 85.1 %gather_fusion.14 = f32[10240]{0:T(1024)S(1)} fusion(f32[5,32,64]{2,1,0:T(8,128)S(1)} %pad_maximum_fusion.1, s32[10240]{0:T(1024)S(1)} %reshape.3230), kind=kCustom, calls=%fused_computation.7.clone | custom fusion | bytes 204800 | tf_op jit(solution)/shard_map/jit(take_along_axis)/gather | solution.py:176
  461.4 42.8 %gather_fusion.13 = f32[5120]{0:T(1024)S(1)} fusion(f32[5,16,64]{2,1,0:T(8,128)S(1)} %reshape.2931, s32[5120]{0:T(1024)S(1)} %reshape.3225), kind=kCustom, calls=%fused_computation.4.clone | custom fusion | bytes 102400 | tf_op jit(solution)/shard_map/jit(take_along_axis)/gather | solution.py:176
  515.6 2.6 scatter_fusion.5
  518.2 2.6 scatter_fusion.6
  520.8 4.4 scatter_fusion.7
  535.4 2.5 fusion.5
  544.3 2.5 gather_fusion.8
  564.7 4.0 collective-permute-start.4
  570.1 43.1 %gather_fusion.15 = f32[5120]{0:T(1024)S(1)} fusion(f32[5,16,64]{2,1,0:T(8,128)S(1)} %bitcast.367, s32[5120]{0:T(1024)S(1)} %reshape.3220), kind=kCustom, calls=%fused_computation.5.clone | custom fusion | bytes 102400 | tf_op jit(solution)/shard_map/jit(take_along_axis)/gather | solution.py:176
  614.2 3.5 all-to-all-start.2
  620.0 85.1 %gather_fusion.17 = f32[10240]{0:T(1024)S(1)} fusion(f32[5,32,64]{2,1,0:T(8,128)S(1)} %pad_maximum_fusion.2, s32[10240]{0:T(1024)S(1)} %reshape.3230), kind=kCustom, calls=%fused_computation.8.clone | custom fusion | bytes 204800 | tf_op jit(solution)/shard_map/jit(take_along_axis)/gather | solution.py:176
  706.4 42.8 %gather_fusion.16 = f32[5120]{0:T(1024)S(1)} fusion(f32[5,16,64]{2,1,0:T(8,128)S(1)} %reshape.2940, s32[5120]{0:T(1024)S(1)} %reshape.3225), kind=kCustom, calls=%fused_computation.6.clone | custom fusion | bytes 102400 | tf_op jit(solution)/shard_map/jit(take_along_axis)/gather | solution.py:176
  (698 shorter events, 192.4 us)
Async XLA Ops:
  6.0 88.2 %collective-permute-start = (f32[5,1,1024]{2,1,0:T(1,128)}, f32[5,1,1024]{2,1,0:T(1,128)}, u32[]{:S(2)}, u32[]{:S(2)}) collective-permute-start(f32[5,1,1024]{2,1,0:T(1,128)} %get-tuple-element.85), channel_id=1, source_target_pairs={{0,4},{4,8},{8,12},{12,16},{16,20},{20,24},{24,28},{1,5},{5,9},{9,... | collective-permute-start | bytes 61448 | tf_op jit(solution)/shard_map/ppermute | solution.py:25
  11.4 83.6 %collective-permute-start.1 = (f32[5,1,1024]{2,1,0:T(1,128)}, f32[5,1,1024]{2,1,0:T(1,128)}, u32[]{:S(2)}, u32[]{:S(2)}) collective-permute-start(f32[5,1,1024]{2,1,0:T(1,128)} %get-tuple-element.86), channel_id=1, source_target_pairs={{4,0},{8,4},{12,8},{16,12},{20,16},{24,20},{28,24},{5,1},{9,5},{13... | collective-permute-start | bytes 61448 | tf_op jit(solution)/shard_map/ppermute | solution.py:28
  13.0 227.5 %copy-start.26 = (s32[16,64]{1,0:T(8,128)}, s32[16,64]{1,0:T(8,128)S(1)}, u32[]{:S(2)}) copy-start(s32[16,64]{1,0:T(8,128)S(1)} %get-tuple-element.13) | copy-start | bytes 12292
  13.0 227.5 %copy-start.39 = (s32[16,64]{1,0:T(8,128)}, s32[16,64]{1,0:T(8,128)S(1)}, u32[]{:S(2)}) copy-start(s32[16,64]{1,0:T(8,128)S(1)} %broadcast_add_fusion.1) | copy-start | bytes 12292
  58.7 189.1 %copy-start.71 = (f32[5,16]{1,0:T(8,128)}, f32[5,16]{1,0:T(8,128)S(1)}, u32[]{:S(2)}) copy-start(f32[5,16]{1,0:T(8,128)S(1)} %fusion.103) | copy-start | bytes 964
  60.1 131.5 %all-to-all-start = ((f32[5,4,512]{2,0,1:T(8,128)}), f32[5,4,512]{2,0,1:T(8,128)}, u32[]{:S(2)}, u32[]{:S(2)}) async-start(f32[5,4,512]{2,0,1:T(8,128)} %copy.374), calls=%async_computation | async-start | bytes 131072 | tf_op jit(solution)/shard_map/all_to_all | solution.py:259
  64.3 125.5 %copy-start.14 = (s32[32,64]{1,0:T(8,128)}, s32[32,64]{1,0:T(8,128)S(1)}, u32[]{:S(2)}) copy-start(s32[32,64]{1,0:T(8,128)S(1)} %multiply_reduce_fusion.6) | copy-start | bytes 24580
  64.3 125.5 %copy-start.23 = (s32[32,64]{1,0:T(8,128)}, s32[32,64]{1,0:T(8,128)S(1)}, u32[]{:S(2)}) copy-start(s32[32,64]{1,0:T(8,128)S(1)} %broadcast_add_fusion) | copy-start | bytes 24580
  64.3 125.5 %copy-start.57 = (pred[32,64]{1,0:T(8,128)(4,1)}, pred[32,64]{1,0:T(8,128)(4,1)S(1)}, u32[]{:S(2)}) copy-start(pred[32,64]{1,0:T(8,128)(4,1)S(1)} %broadcast_compare_fusion) | copy-start | bytes 6148
  296.0 67.9 %collective-permute-start.2 = (f32[5,1,1024]{2,1,0:T(1,128)}, f32[5,1,1024]{2,1,0:T(1,128)}, u32[]{:S(2)}, u32[]{:S(2)}) collective-permute-start(f32[5,1,1024]{2,1,0:T(1,128)} %get-tuple-element.83), channel_id=1, source_target_pairs={{0,4},{4,8},{8,12},{12,16},{16,20},{20,24},{24,28},{1,5},{5,9},{9,... | collective-permute-start | bytes 61448 | tf_op jit(solution)/shard_map/ppermute | solution.py:25
  300.5 64.2 %collective-permute-start.3 = (f32[5,1,1024]{2,1,0:T(1,128)}, f32[5,1,1024]{2,1,0:T(1,128)}, u32[]{:S(2)}, u32[]{:S(2)}) collective-permute-start(f32[5,1,1024]{2,1,0:T(1,128)} %get-tuple-element.84), channel_id=1, source_target_pairs={{4,0},{8,4},{12,8},{16,12},{20,16},{24,20},{28,24},{5,1},{9,5},{13... | collective-permute-start | bytes 61448 | tf_op jit(solution)/shard_map/ppermute | solution.py:28
  349.1 110.8 %all-to-all-start.1 = ((f32[5,4,512]{2,0,1:T(8,128)}), f32[5,4,512]{2,0,1:T(8,128)}, u32[]{:S(2)}, u32[]{:S(2)}) async-start(f32[5,4,512]{2,0,1:T(8,128)} %copy.395), calls=%async_computation.1 | async-start | bytes 131072 | tf_op jit(solution)/shard_map/all_to_all | solution.py:259
  365.7 85.3 %copy-start.63 = (f32[3,32]{0,1:T(8,128)S(1)}, f32[3,32]{0,1:T(8,128)}, u32[]{:S(2)}) copy-start(f32[3,32]{0,1:T(8,128)} %copy.380) | copy-start | bytes 1156
  365.7 88.1 %copy-start.146 = (f32[32]{0:T(128)S(1)}, f32[32]{0:T(128)}, u32[]{:S(2)}) copy-start(f32[32]{0:T(128)} %get-tuple-element.102) | copy-start | bytes 388
  564.7 54.9 %collective-permute-start.4 = (f32[5,1,1024]{2,1,0:T(1,128)S(1)}, f32[5,1,1024]{2,1,0:T(1,128)S(1)}, u32[]{:S(2)}, u32[]{:S(2)}) collective-permute-start(f32[5,1,1024]{2,1,0:T(1,128)S(1)} %get-tuple-element.81), channel_id=1, source_target_pairs={{0,4},{4,8},{8,12},{12,16},{16,20},{20,24},{24,28},{1,5},{5,9},{9,... | collective-permute-start | bytes 61448 | tf_op jit(solution)/shard_map/ppermute | solution.py:25
  568.7 51.0 %collective-permute-start.5 = (f32[5,1,1024]{2,1,0:T(1,128)S(1)}, f32[5,1,1024]{2,1,0:T(1,128)S(1)}, u32[]{:S(2)}, u32[]{:S(2)}) collective-permute-start(f32[5,1,1024]{2,1,0:T(1,128)S(1)} %get-tuple-element.82), channel_id=1, source_target_pairs={{4,0},{8,4},{12,8},{16,12},{20,16},{24,20},{28,24},{5,1},{9,5},{13... | collective-permute-start | bytes 61448 | tf_op jit(solution)/shard_map/ppermute | solution.py:28
  614.2 92.0 %all-to-all-start.2 = ((f32[5,4,512]{2,0,1:T(8,128)}), f32[5,4,512]{2,0,1:T(8,128)S(1)}, u32[]{:S(2)}, u32[]{:S(2)}) async-start(f32[5,4,512]{2,0,1:T(8,128)} %copy.415), calls=%async_computation.2 | async-start | bytes 131072 | tf_op jit(solution)/shard_map/all_to_all | solution.py:259
  618.7 86.3 %copy-start.44 = (f32[5,192,64]{1,2,0:T(8,128)}, f32[5,192,64]{1,2,0:T(8,128)S(1)}, u32[]{:S(2)}) copy-start(f32[5,192,64]{1,2,0:T(8,128)S(1)} %get-tuple-element.120) | copy-start | bytes 737284
  619.9 85.3 %copy-start.16 = (s32[32,64]{1,0:T(8,128)S(1)}, s32[32,64]{1,0:T(8,128)}, u32[]{:S(2)}) copy-start(s32[32,64]{1,0:T(8,128)} %copy-done.14) | copy-start | bytes 24580
  619.9 85.4 %copy-start.64 = (f32[3,32]{0,1:T(8,128)S(1)}, f32[3,32]{0,1:T(8,128)}, u32[]{:S(2)}) copy-start(f32[3,32]{0,1:T(8,128)} %copy.380) | copy-start | bytes 1156
  619.9 85.5 %copy-start.149 = (f32[32]{0:T(128)S(1)}, f32[32]{0:T(128)}, u32[]{:S(2)}) copy-start(f32[32]{0:T(128)} %get-tuple-element.103) | copy-start | bytes 388
  619.9 85.5 %copy-start.154 = (f32[32]{0:T(128)S(1)}, f32[32]{0:T(128)}, u32[]{:S(2)}) copy-start(f32[32]{0:T(128)} %get-tuple-element.197) | copy-start | bytes 388
  619.9 85.7 %copy-start.147 = (f32[32]{0:T(128)S(1)}, f32[32]{0:T(128)}, u32[]{:S(2)}) copy-start(f32[32]{0:T(128)} %get-tuple-element.102) | copy-start | bytes 388
  619.9 85.7 %copy-start.148 = (f32[32]{0:T(128)S(1)}, f32[32]{0:T(128)}, u32[]{:S(2)}) copy-start(f32[32]{0:T(128)} %get-tuple-element.104) | copy-start | bytes 388
  (157 other events, 3034.0 us)
where the time goes:
time: 773 us; the launch traced here: 760 us
  local copies, waits for them, and re-layouts  616 us (80%)
  other arithmetic  80 us (10%)
  matrix products  31.3 us (4%)
  starting transfers between devices  29.2 us (4%)
    gather x22, local copies, waits for them, and re-layouts, orient(): jnp.take_along_axis(values, jnp.broadcast_to(gather_index[None], values.s...  515 us
  transfers between devices with their start and end apart: 9, of which 0 were waited for; matrix products, arithmetic and copies ran while one was open for 60% of the time, Pallas kernels for 0%

commit v1 on v0

v1 whole, which is shorter than its diff:
```python
import functools

import jax
import jax.numpy as jnp
import ml_dtypes
import numpy as np
from jax import lax
from jax.experimental import pallas as pl
from jax.experimental.pallas import tpu as pltpu
from jax.sharding import PartitionSpec as P

time_step = 0.002
half_type = jnp.bfloat16
MESH = pl.DeviceIdType.MESH
inner_nodes = [
    -0.8717401485096066,
    -0.5917001814331423,
    -0.20929921790247888,
    0.20929921790247888,
    0.5917001814331423,
    0.8717401485096066,
]


def legendre_seven(abscissa):
    before = abscissa * 0.0 + 1.0
    current = abscissa + 0.0
    for order in range(1, 7):
        before, current = (
            current,
            ((2 * order + 1) * abscissa * current - order * before) / (order + 1),
        )
    return current


def two_parts(matrix):
    high = matrix.astype(ml_dtypes.bfloat16)
    low = (matrix - high.astype(np.float64)).astype(ml_dtypes.bfloat16)
    return high, low


def tables():
    points = np.array([-1.0] + inner_nodes + [1.0])
    values = legendre_seven(points)
    weights = 2.0 / (56 * values**2)
    deriv = np.zeros((8, 8))
    for row in range(8):
        for col in range(8):
            if row != col:
                deriv[row, col] = values[row] / (values[col] * (points[row] - points[col]))
    deriv[0, 0] = -14.0
    deriv[7, 7] = 14.0
    halves = []
    projections = []
    for side in range(2):
        targets = (points + 2.0 * side - 1.0) / 2.0
        interp = np.ones((8, 8))
        for col in range(8):
            for other in range(8):
                if other != col:
                    interp[:, col] *= (targets - points[other]) / (points[col] - points[other])
        halves.append(interp)
        projections.append(0.5 * (interp.T * weights[None, :]) / weights[:, None])
    pairs = [(a, b) for a in range(2) for b in range(2)]
    mortar = [np.kron(halves[a], halves[b]) for a, b in pairs]
    project = [np.kron(projections[a], projections[b]) for a, b in pairs]
    turn = np.zeros((8, 64, 64))
    for code in range(8):
        for s in range(8):
            for t in range(8):
                a, c = (t, s) if code & 4 else (s, t)
                a = 7 - a if code & 1 else a
                c = 7 - c if code & 2 else c
                turn[code, 8 * s + t, 8 * a + c] = 1.0
    eye = np.eye(64)
    send = mortar + [eye] + [turn[o].T for o in range(8)] + [np.zeros((64, 64))]
    send += [0.25 * eye - q @ m for q, m in zip(project, mortar)]
    take = [turn[o] for o in range(8)] + project + [eye, np.zeros((64, 64))]

    def stacked(mats):
        wide = np.concatenate([m.T for m in mats], axis=1)
        high, low = two_parts(wide)
        return np.concatenate([high, high, low, np.zeros_like(low)], axis=0)

    pick = np.zeros((512, 256))
    for s in range(8):
        for t in range(8):
            column = 8 * s + t
            pick[64 * s + t, column] = 1.0
            pick[64 * s + 8 * t, 64 + column] = 1.0
            pick[64 * s + 56 + t, 128 + column] = 1.0
            pick[64 * s + 8 * t + 7, 192 + column] = 1.0
    along_x = np.concatenate(two_parts(np.kron(deriv.T, np.eye(64))), axis=0)
    along_y = np.concatenate(two_parts(np.kron(np.eye(4), np.kron(deriv.T, np.eye(8)))), axis=0)
    along_z = np.concatenate(two_parts(np.kron(np.eye(32), deriv.T)), axis=0)
    return [
        jnp.asarray(m.astype(ml_dtypes.bfloat16))
        for m in (
            pick,
            pick.T,
            stacked(send),
            stacked(take),
            along_x,
            along_y,
            along_z,
        )
    ]


def dot(left, right):
    return jnp.dot(left, right, preferred_element_type=jnp.float32)


def split(value):
    high = value.astype(half_type)
    return high, (value - high.astype(jnp.float32)).astype(half_type)


def div_five(value):
    return (value * 52429) >> 18


def div_six(value):
    return (value * 43691) >> 18


def swap_halves(value):
    return pltpu.roll(value, 64, axis=1)


def section_kernel(
    sizes,
    state_ref,
    levels_ref,
    send_faces_ref,
    send_counts_ref,
    recv_faces_ref,
    recv_orients_ref,
    recv_counts_ref,
    curve_faces_ref,
    curve_orients_ref,
    curve_counts_ref,
    pick_ref,
    spread_ref,
    send_mat_ref,
    take_mat_ref,
    along_x_ref,
    along_y_ref,
    along_z_ref,
    out_ref,
    tile_out,
    tile_in,
    curve_out,
    curve_in,
    tile_send_sem,
    tile_recv_sem,
    curve_send_sem,
    curve_recv_sem,
):
    curves, tiles, elements, cap_tile, cap_curve, half_rows = sizes
    block = 2 * half_rows
    tile_rows = tiles * block
    curve_rows = 2 * cap_curve
    b = lax.axis_index("curve")
    t = lax.axis_index("tile")
    to_peer = [lax.rem(t + off, tiles) for off in range(tiles)]
    from_peer = [lax.rem(t + tiles - off, tiles) for off in range(tiles)]
    has_prev = b > 0
    has_next = b < curves - 1

    barrier = pltpu.get_barrier_semaphore()
    for off in range(1, tiles):
        pl.semaphore_signal(barrier, inc=1, device_id=(b, to_peer[off]), device_id_type=MESH)

    @pl.when(has_prev)
    def _():
        pl.semaphore_signal(barrier, inc=1, device_id=(b - 1, t), device_id_type=MESH)

    @pl.when(has_next)
    def _():
        pl.semaphore_signal(barrier, inc=1, device_id=(b + 1, t), device_id_type=MESH)

    @pl.when(jnp.logical_not(has_prev))
    def _():
        curve_in[:, 0] = jnp.zeros_like(curve_in[:, 0])

    @pl.when(jnp.logical_not(has_next))
    def _():
        curve_in[:, 1] = jnp.zeros_like(curve_in[:, 1])

    def send_key(peer, slot):
        if slot >= cap_tile:
            return jnp.int32(-1)
        return jnp.where(slot < send_counts_ref[peer], send_faces_ref[peer, slot] * 16, -1)

    def recv_key(peer, slot):
        if slot >= cap_tile:
            return jnp.int32(-1)
        value = recv_faces_ref[peer, slot] * 16 + recv_orients_ref[peer, slot]
        return jnp.where(slot < recv_counts_ref[peer], value, -1)

    def curve_key(side, slot):
        value = curve_faces_ref[side, slot] * 16 + curve_orients_ref[side, slot]
        return jnp.where(slot < curve_counts_ref[side], value, -1)

    out_keys = []
    in_keys = []
    for off in range(tiles):
        out_keys += [send_key(to_peer[off], slot) for slot in range(half_rows)]
        out_keys += [recv_key(to_peer[off], slot) for slot in range(half_rows)]
        in_keys += [recv_key(from_peer[off], slot) for slot in range(half_rows)]
        in_keys += [send_key(from_peer[off], slot) for slot in range(half_rows)]
    rim_keys = [curve_key(side, slot) for side in range(2) for slot in range(cap_curve)]

    sub_iota = lax.broadcasted_iota(jnp.int32, (8, 128), 0)

    def down_rows(keys):
        blocks = []
        for start in range(0, len(keys), 8):
            value = jnp.full((8, 128), -1, jnp.int32)
            for at in range(8):
                value = jnp.where(sub_iota == at, keys[start + at], value)
            blocks.append(value)
        return jnp.concatenate(blocks, axis=0)

    def along_lanes(keys):
        lane = lax.broadcasted_iota(jnp.int32, (8, len(keys)), 1)
        value = jnp.full((8, len(keys)), -1, jnp.int32)
        for at, key in enumerate(keys):
            value = jnp.where(lane == at, key, value)
        return jnp.concatenate([value] * (elements // 8), axis=0)

    def decode(keys, from_send):
        live = keys >= 0
        raw = jnp.maximum(keys, 0) >> 4
        turned = jnp.maximum(keys, 0) & 15
        face_id = jnp.where(from_send, div_five(raw), raw)
        child = raw - 5 * face_id
        element = div_six(face_id)
        face = face_id - 6 * element
        return jnp.where(live, element, -1), face, child, turned

    def half_flags(shape, axis, first):
        at = lax.broadcasted_iota(jnp.int32, shape, axis)
        return (at & (block - 1)) < half_rows if first else (at & (block - 1)) >= half_rows

    lane_t = lax.broadcasted_iota(jnp.int32, (tile_rows, 128), 1)
    low_t = lane_t < 64
    out_is_send = half_flags((tile_rows, 128), 0, True)
    in_is_send = half_flags((tile_rows, 128), 0, False)
    out_elem, out_face, out_child, out_turn = decode(down_rows(out_keys), out_is_send)
    in_elem, in_face, in_child, in_turn = decode(down_rows(in_keys), in_is_send)
    out_y = out_face < 4
    in_y = in_face < 4
    out_code = jnp.where(out_is_send, out_child, 5 + out_turn)
    in_code = jnp.where(in_is_send, 8 + in_child, in_turn)
    upper_t = jnp.where(low_t, 0, 1)
    out_masks = [jnp.where(out_code == 2 * j + upper_t, 1.0, 0.0) for j in range(7)]
    extra_masks = [
        jnp.where(jnp.logical_and(out_is_send, out_code == 2 * j + upper_t), 1.0, 0.0)
        for j in range(2)
    ]
    out_sign = jnp.where(out_is_send, -1.0, 1.0)
    in_sign_half = jnp.where(in_is_send, 0.5, -0.5)
    out_match = low_t == out_y
    in_match = low_t == in_y
    in_low_faces = jnp.where(jnp.logical_and(in_match, jnp.logical_not(in_is_send)), 1.0, 0.0)
    in_high_faces = jnp.where(jnp.logical_and(in_match, in_is_send), 1.0, 0.0)
    out_high_faces = jnp.where(jnp.logical_and(out_match, out_is_send), 1.0, 0.0)

    rim_row = lax.broadcasted_iota(jnp.int32, (curve_rows, 128), 0)
    lane_c = lax.broadcasted_iota(jnp.int32, (curve_rows, 128), 1)
    low_c = lane_c < 64
    rim_elem, _, _, rim_turn = decode(down_rows(rim_keys), rim_row < 0)
    rim_first = rim_row < cap_curve
    rim_match = low_c == rim_first
    rim_sign = jnp.where(rim_first, 1.0, -1.0)
    both_codes = jnp.concatenate([in_code, rim_turn], axis=0)
    upper_b = jnp.where(lax.broadcasted_iota(jnp.int32, both_codes.shape, 1) < 64, 0, 1)
    both_masks = [jnp.where(both_codes == 2 * j + upper_b, 1.0, 0.0) for j in range(7)]
    rim_place = jnp.where(rim_match, 1.0, 0.0)

    def one_hot(flags):
        return jnp.where(flags, 1.0, 0.0).astype(half_type)

    gather_lane = lax.broadcasted_iota(jnp.int32, (tile_rows, 2 * elements), 1) % elements
    out_gather = one_hot(gather_lane == out_elem[:, : 2 * elements])
    rim_lane = lax.broadcasted_iota(jnp.int32, (curve_rows, 2 * elements), 1) % elements
    rim_gather = one_hot(rim_lane == rim_elem[:, : 2 * elements])

    lane_shape = (elements, 4 * tile_rows)
    lane_s = lax.broadcasted_iota(jnp.int32, lane_shape, 1)
    in_part = lane_s < 2 * tile_rows
    first_half = (lane_s & (block - 1)) < half_rows
    lane_from_send = first_half != in_part
    t_elem, t_face, _, _ = decode(along_lanes(in_keys * 2 + out_keys * 2), lane_from_send)
    t_hit = t_elem == lax.broadcasted_iota(jnp.int32, lane_shape, 0)
    tile_scatter = one_hot(t_hit)
    rim_shape = (elements, 2 * curve_rows)
    c_elem, c_face, _, _ = decode(
        along_lanes(rim_keys * 2), lax.broadcasted_iota(jnp.int32, rim_shape, 1) < 0
    )
    c_hit = c_elem == lax.broadcasted_iota(jnp.int32, rim_shape, 0)
    rim_scatter = one_hot(c_hit)

    def any_lane(flags):
        return jnp.max(jnp.where(flags, 1.0, 0.0), axis=1, keepdims=True)

    listed = [any_lane(jnp.logical_and(c_hit, c_face == f)) for f in (0, 1)]
    listed += [any_lane(jnp.logical_and(t_hit, t_face == f)) for f in (2, 3, 4, 5)]

    scale_blocks = []
    for start in range(0, elements, 8):
        value = jnp.zeros((8, 128), jnp.int32)
        for at in range(8):
            value = jnp.where(sub_iota == at, jnp.int32(1) << levels_ref[start + at], value)
        scale_blocks.append(value.astype(jnp.float32))
    scale = jnp.concatenate(scale_blocks, axis=0)
    scale = jnp.concatenate([scale] * 4, axis=1)
    vol_scale = scale * (-time_step)
    lift = scale * (28.0 * time_step)

    node = lax.broadcasted_iota(jnp.int32, (elements, 512), 1)
    vel_to_sum = []
    pres_to_vel = []
    own_damp = []
    side_damp = []
    for dim in range(3):
        place = (node >> (6 - 3 * dim)) & 7
        low_end = place == 0
        high_end = place == 7
        on_face = jnp.logical_or(low_end, high_end)
        known = jnp.where(low_end, listed[2 * dim], listed[2 * dim + 1])
        strong = jnp.where(on_face, lift * (1.0 - 0.5 * known), 0.0)
        weak = jnp.where(on_face, lift * (0.5 * known), 0.0)
        vel_to_sum.append(jnp.where(low_end, -strong, strong))
        pres_to_vel.append(jnp.where(low_end, -weak, weak))
        own_damp.append(strong)
        side_damp.append(weak)
    total_damp = side_damp[0] + side_damp[1] + side_damp[2]
    vel_damp = [own_damp[d] + (total_damp - side_damp[d]) for d in range(3)]

    def tile_copies(stage):
        return [
            pltpu.make_async_remote_copy(
                src_ref=tile_out.at[stage, off],
                dst_ref=tile_in.at[stage, off],
                send_sem=tile_send_sem.at[stage, off],
                recv_sem=tile_recv_sem.at[stage, off],
                device_id=(b, to_peer[off]),
                device_id_type=MESH,
            )
            for off in range(1, tiles)
        ]

    def curve_copy(stage, side):
        return pltpu.make_async_remote_copy(
            src_ref=curve_out.at[stage, side],
            dst_ref=curve_in.at[stage, 1 - side],
            send_sem=curve_send_sem.at[stage, side],
            recv_sem=curve_recv_sem.at[stage, 1 - side],
            device_id=(b - 1 + 2 * side, t),
            device_id_type=MESH,
        )

    def packed(first, second, low):
        return jnp.where(low, first, second)

    def pair_rows(value, low):
        high = value.astype(half_type).astype(jnp.float32)
        return jnp.concatenate([jnp.where(low, high, value - high), high], axis=1).astype(half_type)

    def rates(current, stage):
        parts = [split(value) for value in current]
        highs = [part[0] for part in parts]
        lows = [part[1] for part in parts]

        low_e = lax.broadcasted_iota(jnp.int32, (elements, 128), 1) < 64
        ends = [split(jnp.where(low_e, v[:, :128], v[:, 384:])) for v in current]
        ends = jnp.concatenate([jnp.concatenate(e, axis=0) for e in ends], axis=1)
        rim = dot(rim_gather, ends)
        rim_vals = []
        for f in range(5):
            kept = jnp.where(rim_match, rim[:, 128 * f : 128 * f + 128], 0.0)
            rim_vals.append(kept + swap_halves(kept))
        sum_part = rim_sign * rim_vals[1] - rim_vals[0]
        vel_part = rim_sign * rim_vals[4] - rim_vals[1]
        rim_send = jnp.concatenate(
            [packed(sum_part, vel_part, low_c), packed(rim_vals[2], rim_vals[3], low_c)], axis=1
        )
        curve_out[stage] = rim_send.reshape(2, cap_curve, 256)
        if stage == 0:
            pl.semaphore_wait(
                barrier, tiles - 1 + has_prev.astype(jnp.int32) + has_next.astype(jnp.int32)
            )

        @pl.when(has_prev)
        def _():
            curve_copy(stage, 0).start()

        @pl.when(has_next)
        def _():
            curve_copy(stage, 1).start()

        traces = dot(jnp.concatenate(highs + lows, axis=0), pick_ref[...]).astype(half_type)
        columns = []
        for f in range(5):
            at = f * elements
            low_at = (5 + f) * elements
            columns.append(
                jnp.concatenate(
                    [traces[at : at + elements], traces[low_at : low_at + elements]], axis=0
                )
            )
        own = dot(out_gather, jnp.concatenate(columns, axis=1))
        own_rows = []
        for f in range(5):
            side = jnp.where(
                out_is_send, own[:, 256 * f + 128 : 256 * f + 256], own[:, 256 * f : 256 * f + 128]
            )
            kept = jnp.where(out_match, side, 0.0)
            own_rows.append(pair_rows(kept + swap_halves(kept), low_t))
        coded = dot(jnp.concatenate(own_rows, axis=0), send_mat_ref[...])

        def choose(source, rows_at, rows, masks, first):
            total = None
            for j, mask in enumerate(masks):
                at = 128 * (first + j)
                term = mask * source[rows_at : rows_at + rows, at : at + 128]
                total = term if total is None else total + term
            return total + swap_halves(total)

        mortar = [choose(coded, f * tile_rows, tile_rows, out_masks, 0) for f in range(5)]
        normal = jnp.where(out_y, mortar[2], mortar[3])
        other = jnp.where(out_y, mortar[3], mortar[2])
        sum_part = out_sign * normal - mortar[0]
        vel_part = out_sign * mortar[4] - normal
        tile_send = jnp.concatenate(
            [packed(sum_part, vel_part, low_t), packed(mortar[1], other, low_t)], axis=1
        )
        tile_send = tile_send.reshape(tiles, block, 256)
        tile_out[stage] = tile_send
        tile_in[stage, 0] = tile_send[0]
        copies = tile_copies(stage)
        for copy in copies:
            copy.start()

        rest = [choose(coded, f * tile_rows, tile_rows, extra_masks, 7) for f in range(5)]
        rest_n = jnp.where(out_y, rest[2], rest[3])
        rest_o = jnp.where(out_y, rest[3], rest[2])
        rest_p = 0.5 * (rest[4] + rest_n)
        rest_n = 0.5 * (rest_n + rest[4])
        rest_o = 0.5 * rest_o
        rest_fields = [
            0.5 * (rest[0] + jnp.where(out_y, rest[2], rest[3])),
            0.5 * rest[1],
            jnp.where(out_y, rest_n, rest_o),
            jnp.where(out_y, rest_o, rest_n),
            rest_p,
        ]
        rest_parts = [split(value * out_high_faces) for value in rest_fields]

        grad = dot(
            jnp.concatenate([highs[1], highs[4], lows[1], lows[4]], axis=0), along_x_ref[:512]
        )
        n2 = 2 * elements
        grad_x = grad[:n2] + grad[n2:]
        grad_x = grad_x + dot(jnp.concatenate([highs[1], highs[4]], axis=0), along_x_ref[512:])

        def halves(f, source):
            return [source[f][:, :256], source[f][:, 256:]]

        def banded(f, mat_ref):
            high_rows = jnp.concatenate(halves(f, highs) + halves(4, highs), axis=0)
            low_rows = jnp.concatenate(halves(f, lows) + halves(4, lows), axis=0)
            first = dot(jnp.concatenate([high_rows, low_rows], axis=0), mat_ref[:256])
            n4 = 4 * elements
            total = first[:n4] + first[n4:] + dot(high_rows, mat_ref[256:])
            vel = jnp.concatenate([total[:elements], total[elements:n2]], axis=1)
            pres = jnp.concatenate([total[n2 : 3 * elements], total[3 * elements :]], axis=1)
            return vel, pres

        vel_y, pres_y = banded(2, along_y_ref)
        vel_z, pres_z = banded(3, along_z_ref)
        diverge = vol_scale * (grad_x[:elements] + vel_y + vel_z)
        to_sum = diverge
        for d in range(3):
            to_sum = to_sum + vel_to_sum[d] * current[1 + d]
        pres_grads = (grad_x[elements:], pres_y, pres_z)
        result = [to_sum - total_damp * current[0]]
        for d in range(3):
            result.append(
                vol_scale * pres_grads[d]
                + pres_to_vel[d] * current[4]
                - vel_damp[d] * current[1 + d]
            )
        result.append(to_sum - total_damp * current[4])

        for copy in copies:
            copy.wait()

        @pl.when(has_prev)
        def _():
            copy = curve_copy(stage, 0)
            copy.wait_send()
            curve_copy(stage, 1).wait_recv()

        @pl.when(has_next)
        def _():
            copy = curve_copy(stage, 1)
            copy.wait_send()
            curve_copy(stage, 0).wait_recv()

        arrived = jnp.concatenate(
            [
                tile_in[stage].reshape(tile_rows, 256),
                curve_in[stage].reshape(curve_rows, 256),
            ],
            axis=0,
        )
        rows = tile_rows + curve_rows
        low_b = lax.broadcasted_iota(jnp.int32, (rows, 128), 1) < 64
        fields = []
        for at in range(2):
            value = arrived[:, 128 * at : 128 * at + 128]
            turned = swap_halves(value)
            fields.append(pair_rows(jnp.where(low_b, value, turned), low_b))
            fields.append(pair_rows(jnp.where(low_b, turned, value), low_b))
        taken = dot(jnp.concatenate(fields, axis=0), take_mat_ref[...])
        chosen = [choose(taken, f * rows, rows, both_masks, 0) for f in range(4)]

        rim_in = [value[tile_rows:] * rim_place for value in chosen]
        rim_cols = [jnp.concatenate(split(value), axis=0) for value in rim_in]
        placed = dot(rim_scatter, jnp.concatenate(rim_cols, axis=1))
        place_sum = -0.5 * placed[:, :128]
        place_vel = -0.5 * placed[:, 128:256]
        place_pres = jnp.where(low_e, place_vel, -place_vel)
        rim_fields = [
            place_sum,
            place_vel,
            0.5 * placed[:, 256:384],
            0.5 * placed[:, 384:512],
            place_pres,
        ]

        tile_vals = [value[:tile_rows] for value in chosen]
        put_sum = -0.5 * tile_vals[0]
        put_n = -0.5 * tile_vals[1]
        put_o = 0.5 * tile_vals[3]
        put = [
            put_sum,
            0.5 * tile_vals[2],
            jnp.where(in_y, put_n, put_o),
            jnp.where(in_y, put_o, put_n),
            in_sign_half * tile_vals[1],
        ]
        zero_part = jnp.zeros((tile_rows, 128), half_type)
        columns = []
        for f in range(5):
            first = split(put[f] * in_low_faces)
            second = split(put[f] * in_high_faces)
            high, low = rest_parts[f]
            columns.append(jnp.concatenate([first[0], first[1], zero_part, zero_part], axis=0))
            columns.append(jnp.concatenate([second[0], second[1], high, low], axis=0))
        on_faces = dot(tile_scatter, jnp.concatenate(columns, axis=1))
        face_parts = [split(on_faces[:, 256 * f : 256 * f + 256]) for f in range(5)]
        spread = dot(
            jnp.concatenate([p[0] for p in face_parts] + [p[1] for p in face_parts], axis=0),
            spread_ref[...],
        )
        finished = []
        zero_middle = jnp.zeros((elements, 256), jnp.float32)
        for f in range(5):
            at = f * elements
            low_at = (5 + f) * elements
            nodes = spread[at : at + elements] + spread[low_at : low_at + elements]
            rim_nodes = jnp.concatenate(
                [
                    jnp.where(low_e, rim_fields[f], 0.0),
                    zero_middle,
                    jnp.where(low_e, 0.0, rim_fields[f]),
                ],
                axis=1,
            )
            finished.append(result[f] + lift * (nodes + rim_nodes))
        return finished

    current = [state_ref[f] for f in range(5)]
    change = rates(current, 0)
    current = [current[f] + change[f] for f in range(5)]
    change = rates(current, 1)
    current = [0.75 * state_ref[f] + 0.25 * (current[f] + change[f]) for f in range(5)]
    change = rates(current, 2)
    for f in range(5):
        out_ref[f] = state_ref[f] / 3.0 + (2.0 / 3.0) * (current[f] + change[f])


def shards(
    state,
    levels,
    send_faces,
    send_counts,
    recv_faces,
    recv_orients,
    recv_counts,
    curve_faces,
    curve_orients,
    curve_counts,
):
    curves = lax.axis_size("curve")
    tiles, cap_tile = send_faces.shape
    cap_curve = curve_faces.shape[1]
    elements = state.shape[1]
    half_rows = -(-cap_tile // 4) * 4
    sizes = (curves, tiles, elements, cap_tile, cap_curve, half_rows)
    smem = pl.BlockSpec(memory_space=pltpu.SMEM)
    vmem = pl.BlockSpec(memory_space=pltpu.VMEM)
    block = 2 * half_rows
    return pl.pallas_call(
        functools.partial(section_kernel, sizes),
        out_shape=jax.ShapeDtypeStruct(state.shape, state.dtype),
        in_specs=[vmem] + [smem] * 9 + [vmem] * 7,
        out_specs=vmem,
        scratch_shapes=[
            pltpu.VMEM((3, tiles, block, 256), jnp.float32),
            pltpu.VMEM((3, tiles, block, 256), jnp.float32),
            pltpu.VMEM((3, 2, cap_curve, 256), jnp.float32),
            pltpu.VMEM((3, 2, cap_curve, 256), jnp.float32),
            pltpu.SemaphoreType.DMA((3, tiles)),
            pltpu.SemaphoreType.DMA((3, tiles)),
            pltpu.SemaphoreType.DMA((3, 2)),
            pltpu.SemaphoreType.DMA((3, 2)),
        ],
        compiler_params=pltpu.CompilerParams(
            collective_id=0, has_side_effects=True, vmem_limit_bytes=40 * 1024 * 1024
        ),
    )(
        state,
        levels,
        send_faces,
        send_counts,
        recv_faces,
        recv_orients,
        recv_counts,
        curve_faces,
        curve_orients,
        curve_counts,
        *tables(),
    )


def solution(mesh):
    return jax.shard_map(
        shards,
        mesh=mesh,
        in_specs=(
            P(None, ("curve", "tile"), None),
            P(("curve", "tile")),
            P(("curve", "tile"), None),
            P(("curve", "tile")),
            P(("curve", "tile"), None),
            P(("curve", "tile"), None),
            P(("curve", "tile")),
            P(("curve", "tile"), None),
            P(("curve", "tile"), None),
            P(("curve", "tile")),
        ),
        out_specs=P(None, ("curve", "tile"), None),
        check_vma=False,
    )
```

time: 773 us -> 33.5 us (0.04); the launches traced: 760 us -> 33 us
  local copies, waits for them, and re-layouts: 616 us -> 14.8 us
  other arithmetic: 80 us -> 0 us
  matrix products: 31.3 us -> 0 us
  starting transfers between devices: 29.2 us -> 0 us
  Pallas kernels: 0 us -> 18.1 us
    gather x37 -> x0, local copies, waits for them, and re-layouts: 532 us -> none  [the longest x22 515 us: orient(): jnp.take_along_axis(values, jnp.broadcast_to(gather_index[None], values.s...]
    dot_general x21 -> x0, matrix products: 31.3 us -> none  [the longest x6 7.63 us: child_apply(): mapped = jnp.einsum('fnj,cij->cfni', values, matrices, precision=highest)]
    slice x48 -> x0, local copies, waits for them, and re-layouts: 28.6 us -> none  [the longest x9 8.24 us: wall_state(): own_side[:1]]
    scatter-add x12 -> x0, other arithmetic: 25.1 us -> none  [the longest x3 10.4 us: rhs(): accumulated = accumulated.at[:, curve_ids].add(curve_flux)]
    mul x24 -> x0, other arithmetic: 20.6 us -> none  [the longest x3 4.47 us: rhs(): (normal_flux(traces, all_faces) - flux_star) * face_scales[None, :, None]]
    pallas_call x0 -> x1, Pallas kernels: none -> 18.1 us  [shards(): pl.pallas_call(functools.partial(section_kernel, sizes), out_shape=jax.Sh...]
    ppermute x6 -> x0, starting transfers between devices: 17.8 us -> none  [the longest x3 13.9 us: with_halo(): lax.ppermute(lax.slice_in_dim(block, block.shape[dim] - width, None, axis...]
    reshape x27 -> x0, local copies, waits for them, and re-layouts: 14.8 us -> none  [the longest x9 11.8 us: face_traces(): return flat.reshape(fields, elements * 6, 64)]
  transfers between devices with their start and end apart: 9 -> 0, of which waited for: 0 -> 0; matrix products, arithmetic and copies ran while one was open for 60% -> 0% of each run, Pallas kernels for 0% -> 0%
where the time goes in v1:
time: 33.5 us; the launch traced here: 33 us
  Pallas kernels  18.1 us (54%)
  local copies, waits for them, and re-layouts  14.8 us (44%)
    pallas_call x1, Pallas kernels, shards(): pl.pallas_call(functools.partial(section_kernel, sizes), out_shape=jax.Sh...  18.1 us
    unnamed x35, local copies, waits for them, and re-layouts  14.8 us

profile of v1, /device:TPU:0, one launch (start us, length us, event | category | flops | bytes accessed | tf_op | source)
XLA Modules:
  0.0 33.0 jit_solution(3975218500617466319)
XLA Ops:
  0.0 0.0 copy-start
  0.0 1.2 %copy-done = bf16[1024,512]{1,0:T(8,128)(2,1)S(1)} copy-done((bf16[1024,512]{1,0:T(8,128)(2,1)S(1)}, bf16[1024,512]{1,0:T(8,128)(2,1)}, u32[]{:S(2)}) %copy-start) | copy-done | bytes 1048600
  1.2 0.0 copy-start.1
  1.2 1.1 %copy-done.1 = bf16[256,1152]{1,0:T(8,128)(2,1)S(1)} copy-done((bf16[256,1152]{1,0:T(8,128)(2,1)S(1)}, bf16[256,1152]{1,0:T(8,128)(2,1)}, u32[]{:S(2)}) %copy-start.1) | copy-done | bytes 589848
  2.3 0.0 copy-start.2
  2.3 1.0 %copy-done.2 = bf16[256,896]{1,0:T(8,128)(2,1)S(1)} copy-done((bf16[256,896]{1,0:T(8,128)(2,1)S(1)}, bf16[256,896]{1,0:T(8,128)(2,1)}, u32[]{:S(2)}) %copy-start.2) | copy-done | bytes 458776
  3.3 0.0 copy-start.3
  3.3 1.0 %copy-done.3 = f32[5,32,512]{2,1,0:T(8,128)S(1)} copy-done((f32[5,32,512]{2,1,0:T(8,128)S(1)}, f32[5,32,512]{2,1,0:T(8,128)}, u32[]{:S(2)}) %copy-start.3) | copy-done | bytes 327704
  4.3 0.9 %copy-done.4 = bf16[512,256]{1,0:T(8,128)(2,1)S(1)} copy-done((bf16[512,256]{1,0:T(8,128)(2,1)S(1)}, bf16[512,256]{1,0:T(8,128)(2,1)}, u32[]{:S(2)}) %copy-start.4) | copy-done | bytes 262168
  5.2 0.0 copy-start.5
  5.2 0.9 %copy-done.5 = bf16[512,256]{1,0:T(8,128)(2,1)S(1)} copy-done((bf16[512,256]{1,0:T(8,128)(2,1)S(1)}, bf16[512,256]{1,0:T(8,128)(2,1)}, u32[]{:S(2)}) %copy-start.5) | copy-done | bytes 262168
  6.2 0.9 %copy-done.6 = bf16[256,512]{1,0:T(8,128)(2,1)S(1)} copy-done((bf16[256,512]{1,0:T(8,128)(2,1)S(1)}, bf16[256,512]{1,0:T(8,128)(2,1)}, u32[]{:S(2)}) %copy-start.6) | copy-done | bytes 262168
  7.1 0.9 %copy-done.7 = bf16[512,256]{1,0:T(8,128)(2,1)S(1)} copy-done((bf16[512,256]{1,0:T(8,128)(2,1)S(1)}, bf16[512,256]{1,0:T(8,128)(2,1)}, u32[]{:S(2)}) %copy-start.7) | copy-done | bytes 262168
  8.1 0.7 %copy-done.8 = s32[4,4]{1,0:T(4,128)S(1)} copy-done((s32[4,4]{1,0:T(4,128)S(1)}, s32[4,4]{1,0:T(4,128)}, u32[]{:S(2)}) %copy-start.8) | copy-done | bytes 88
  8.8 0.7 %copy-done.9 = s32[4,4]{1,0:T(4,128)S(1)} copy-done((s32[4,4]{1,0:T(4,128)S(1)}, s32[4,4]{1,0:T(4,128)}, u32[]{:S(2)}) %copy-start.9) | copy-done | bytes 88
  9.5 0.7 %copy-done.10 = s32[4,4]{1,0:T(4,128)S(1)} copy-done((s32[4,4]{1,0:T(4,128)S(1)}, s32[4,4]{1,0:T(4,128)}, u32[]{:S(2)}) %copy-start.10) | copy-done | bytes 88
  10.1 0.7 %copy-done.11 = s32[2,16]{1,0:T(2,128)S(1)} copy-done((s32[2,16]{1,0:T(2,128)S(1)}, s32[2,16]{1,0:T(2,128)}, u32[]{:S(2)}) %copy-start.11) | copy-done | bytes 152
  10.8 0.7 %copy-done.12 = s32[2,16]{1,0:T(2,128)S(1)} copy-done((s32[2,16]{1,0:T(2,128)S(1)}, s32[2,16]{1,0:T(2,128)}, u32[]{:S(2)}) %copy-start.12) | copy-done | bytes 152
  11.5 0.7 %copy-done.13 = s32[32]{0:T(128)S(1)} copy-done((s32[32]{0:T(128)S(1)}, s32[32]{0:T(128)}, u32[]{:S(2)}) %copy-start.13) | copy-done | bytes 152
  12.1 0.7 %copy-done.14 = s32[4]{0:T(128)S(1)} copy-done((s32[4]{0:T(128)S(1)}, s32[4]{0:T(128)}, u32[]{:S(2)}) %copy-start.14) | copy-done | bytes 40
  12.8 0.7 %copy-done.15 = s32[4]{0:T(128)S(1)} copy-done((s32[4]{0:T(128)S(1)}, s32[4]{0:T(128)}, u32[]{:S(2)}) %copy-start.15) | copy-done | bytes 40
  13.5 0.7 %copy-done.16 = s32[2]{0:T(128)S(1)} copy-done((s32[2]{0:T(128)S(1)}, s32[2]{0:T(128)}, u32[]{:S(2)}) %copy-start.16) | copy-done | bytes 32
  14.1 18.1 %shard_map.163 = f32[5,32,512]{2,1,0:T(8,128)S(1)} custom-call(f32[5,32,512]{2,1,0:T(8,128)S(1)} %copy-done.3, s32[32]{0:T(128)S(1)} %copy-done.13, s32[4,4]{1,0:T(4,128)S(1)} %copy-done.8, s32[4]{0:T(128)S(1)} %copy-done.14, s32[4,4]{1,0:T(4,128)S(1)} %copy-done.9, s32[4,4]{1,0:T(4,128)S(1)} %copy-done.10, s32[4]{0:T(128)S(1)} %copy-done.15, ...), custom_call_target="tpu_custom_call" | custom-call | tf_op jit(solution)/shard_map/pallas_call | solution.py:619
  32.3 0.7 %copy.19 = f32[5,32,512]{2,1,0:T(8,128)} copy(f32[5,32,512]{2,1,0:T(8,128)S(1)} %shard_map.163) | data formatting | bytes 655360
  (12 shorter events, 0.0 us)
Async XLA Ops:
  0.0 1.2 %copy-start = (bf16[1024,512]{1,0:T(8,128)(2,1)S(1)}, bf16[1024,512]{1,0:T(8,128)(2,1)}, u32[]{:S(2)}) copy-start(bf16[1024,512]{1,0:T(8,128)(2,1)} %constant.18.clone.along_x_ref) | copy-start | bytes 3145732
  1.2 1.1 %copy-start.1 = (bf16[256,1152]{1,0:T(8,128)(2,1)S(1)}, bf16[256,1152]{1,0:T(8,128)(2,1)}, u32[]{:S(2)}) copy-start(bf16[256,1152]{1,0:T(8,128)(2,1)} %constant.16.clone.send_mat_ref) | copy-start | bytes 1769476
  2.3 1.0 %copy-start.2 = (bf16[256,896]{1,0:T(8,128)(2,1)S(1)}, bf16[256,896]{1,0:T(8,128)(2,1)}, u32[]{:S(2)}) copy-start(bf16[256,896]{1,0:T(8,128)(2,1)} %constant.17.clone.take_mat_ref) | copy-start | bytes 1376260
  3.3 1.0 %copy-start.3 = (f32[5,32,512]{2,1,0:T(8,128)S(1)}, f32[5,32,512]{2,1,0:T(8,128)}, u32[]{:S(2)}) copy-start(f32[5,32,512]{2,1,0:T(8,128)} %state_ref.1) | copy-start | bytes 983044
  4.3 0.9 %copy-start.4 = (bf16[512,256]{1,0:T(8,128)(2,1)S(1)}, bf16[512,256]{1,0:T(8,128)(2,1)}, u32[]{:S(2)}) copy-start(bf16[512,256]{1,0:T(8,128)(2,1)} %constant.20.clone.along_z_ref) | copy-start | bytes 786436
  5.2 0.9 %copy-start.5 = (bf16[512,256]{1,0:T(8,128)(2,1)S(1)}, bf16[512,256]{1,0:T(8,128)(2,1)}, u32[]{:S(2)}) copy-start(bf16[512,256]{1,0:T(8,128)(2,1)} %constant.19.clone.along_y_ref) | copy-start | bytes 786436
  6.2 0.9 %copy-start.6 = (bf16[256,512]{1,0:T(8,128)(2,1)S(1)}, bf16[256,512]{1,0:T(8,128)(2,1)}, u32[]{:S(2)}) copy-start(bf16[256,512]{1,0:T(8,128)(2,1)} %constant.15.clone.spread_ref) | copy-start | bytes 786436
  7.1 0.9 %copy-start.7 = (bf16[512,256]{1,0:T(8,128)(2,1)S(1)}, bf16[512,256]{1,0:T(8,128)(2,1)}, u32[]{:S(2)}) copy-start(bf16[512,256]{1,0:T(8,128)(2,1)} %constant.14.clone.pick_ref) | copy-start | bytes 786436
  8.1 0.7 %copy-start.8 = (s32[4,4]{1,0:T(4,128)S(1)}, s32[4,4]{1,0:T(4,128)}, u32[]{:S(2)}) copy-start(s32[4,4]{1,0:T(4,128)} %send_faces_ref.1) | copy-start | bytes 196
  8.8 0.7 %copy-start.9 = (s32[4,4]{1,0:T(4,128)S(1)}, s32[4,4]{1,0:T(4,128)}, u32[]{:S(2)}) copy-start(s32[4,4]{1,0:T(4,128)} %recv_faces_ref.1) | copy-start | bytes 196
  9.4 0.7 %copy-start.10 = (s32[4,4]{1,0:T(4,128)S(1)}, s32[4,4]{1,0:T(4,128)}, u32[]{:S(2)}) copy-start(s32[4,4]{1,0:T(4,128)} %recv_orients_ref.1) | copy-start | bytes 196
  10.1 0.7 %copy-start.11 = (s32[2,16]{1,0:T(2,128)S(1)}, s32[2,16]{1,0:T(2,128)}, u32[]{:S(2)}) copy-start(s32[2,16]{1,0:T(2,128)} %curve_faces_ref.1) | copy-start | bytes 388
  10.8 0.7 %copy-start.12 = (s32[2,16]{1,0:T(2,128)S(1)}, s32[2,16]{1,0:T(2,128)}, u32[]{:S(2)}) copy-start(s32[2,16]{1,0:T(2,128)} %curve_orients_ref.1) | copy-start | bytes 388
  11.5 0.7 %copy-start.13 = (s32[32]{0:T(128)S(1)}, s32[32]{0:T(128)}, u32[]{:S(2)}) copy-start(s32[32]{0:T(128)} %levels_ref.1) | copy-start | bytes 388
  12.1 0.7 %copy-start.14 = (s32[4]{0:T(128)S(1)}, s32[4]{0:T(128)}, u32[]{:S(2)}) copy-start(s32[4]{0:T(128)} %send_counts_ref.1) | copy-start | bytes 52
  12.8 0.7 %copy-start.15 = (s32[4]{0:T(128)S(1)}, s32[4]{0:T(128)}, u32[]{:S(2)}) copy-start(s32[4]{0:T(128)} %recv_counts_ref.1) | copy-start | bytes 52
  13.5 0.7 %copy-start.16 = (s32[2]{0:T(128)S(1)}, s32[2]{0:T(128)}, u32[]{:S(2)}) copy-start(s32[2]{0:T(128)} %curve_counts_ref.1) | copy-start | bytes 28

commit v2 on v1

--- a/solution.py
+++ b/solution.py
@@ -12,6 +12,8 @@
 time_step = 0.002
 half_type = jnp.bfloat16
 MESH = pl.DeviceIdType.MESH
+operand_count = 17
+load_order = [3, 2, 5, 4, 6, 8, 7, 9, 1, 0, 10, 12, 14, 15, 16, 13, 11]
 inner_nodes = [
     -0.8717401485096066,
     -0.5917001814331423,
@@ -31,12 +33,6 @@
             ((2 * order + 1) * abscissa * current - order * before) / (order + 1),
         )
     return current
-
-
-def two_parts(matrix):
-    high = matrix.astype(ml_dtypes.bfloat16)
-    low = (matrix - high.astype(np.float64)).astype(ml_dtypes.bfloat16)
-    return high, low
 
 
 def tables():
@@ -77,11 +73,6 @@
     send += [0.25 * eye - q @ m for q, m in zip(project, mortar)]
     take = [turn[o] for o in range(8)] + project + [eye, np.zeros((64, 64))]
 
-    def stacked(mats):
-        wide = np.concatenate([m.T for m in mats], axis=1)
-        high, low = two_parts(wide)
-        return np.concatenate([high, high, low, np.zeros_like(low)], axis=0)
-
     pick = np.zeros((512, 256))
     for s in range(8):
         for t in range(8):
@@ -90,19 +81,16 @@
             pick[64 * s + 8 * t, 64 + column] = 1.0
             pick[64 * s + 56 + t, 128 + column] = 1.0
             pick[64 * s + 8 * t + 7, 192 + column] = 1.0
-    along_x = np.concatenate(two_parts(np.kron(deriv.T, np.eye(64))), axis=0)
-    along_y = np.concatenate(two_parts(np.kron(np.eye(4), np.kron(deriv.T, np.eye(8)))), axis=0)
-    along_z = np.concatenate(two_parts(np.kron(np.eye(32), deriv.T)), axis=0)
     return [
-        jnp.asarray(m.astype(ml_dtypes.bfloat16))
+        jnp.asarray(m.astype(np.float32))
         for m in (
             pick,
             pick.T,
-            stacked(send),
-            stacked(take),
-            along_x,
-            along_y,
-            along_z,
+            np.concatenate([m.T for m in send], axis=1),
+            np.concatenate([m.T for m in take], axis=1),
+            np.kron(deriv.T, np.eye(64)),
+            np.kron(np.eye(4), np.kron(deriv.T, np.eye(8))),
+            np.kron(np.eye(32), deriv.T),
         )
     ]
 
@@ -130,33 +118,43 @@
 
 def section_kernel(
     sizes,
-    state_ref,
-    levels_ref,
-    send_faces_ref,
-    send_counts_ref,
-    recv_faces_ref,
-    recv_orients_ref,
-    recv_counts_ref,
-    curve_faces_ref,
-    curve_orients_ref,
-    curve_counts_ref,
-    pick_ref,
-    spread_ref,
-    send_mat_ref,
-    take_mat_ref,
-    along_x_ref,
-    along_y_ref,
-    along_z_ref,
-    out_ref,
-    tile_out,
-    tile_in,
-    curve_out,
-    curve_in,
-    tile_send_sem,
-    tile_recv_sem,
-    curve_send_sem,
-    curve_recv_sem,
+    *refs,
 ):
+    given = refs[:operand_count]
+    out_ref = refs[operand_count]
+    held = refs[operand_count + 1 : 2 * operand_count + 1]
+    (
+        tile_out,
+        tile_in,
+        curve_out,
+        curve_in,
+        tile_send_sem,
+        tile_recv_sem,
+        curve_send_sem,
+        curve_recv_sem,
+        load_sem,
+        *ready,
+    ) = refs[2 * operand_count + 1 :]
+    pick_ref, spread_ref, send_mat_ref, take_mat_ref, along_x_ref, along_y_ref, along_z_ref = ready
+    (
+        state_ref,
+        levels_ref,
+        send_faces_ref,
+        send_counts_ref,
+        recv_faces_ref,
+        recv_orients_ref,
+        recv_counts_ref,
+        curve_faces_ref,
+        curve_orients_ref,
+        curve_counts_ref,
+        *wide,
+    ) = held
+    loads = [
+        pltpu.make_async_copy(source, target, load_sem.at[at])
+        for at, (source, target) in enumerate(zip(given, held))
+    ]
+    for at in load_order:
+        loads[at].start()
     curves, tiles, elements, cap_tile, cap_curve, half_rows = sizes
     block = 2 * half_rows
     tile_rows = tiles * block
@@ -187,6 +185,9 @@
     @pl.when(jnp.logical_not(has_next))
     def _():
         curve_in[:, 1] = jnp.zeros_like(curve_in[:, 1])
+
+    for at in range(1, 10):
+        loads[at].wait()
 
     def send_key(peer, slot):
         if slot >= cap_tile:
@@ -340,6 +341,17 @@
     total_damp = side_damp[0] + side_damp[1] + side_damp[2]
     vel_damp = [own_damp[d] + (total_damp - side_damp[d]) for d in range(3)]
 
+    def prepare(at):
+        loads[10 + at].wait()
+        value = wide[at][...]
+        high, low = split(value)
+        if at < 2:
+            ready[at][...] = high
+        elif at < 4:
+            ready[at][...] = jnp.concatenate([high, high, low, jnp.zeros_like(low)], axis=0)
+        else:
+            ready[at][...] = jnp.concatenate([high, low], axis=0)
+
     def tile_copies(stage):
         return [
             pltpu.make_async_remote_copy(
@@ -402,6 +414,8 @@
         def _():
             curve_copy(stage, 1).start()
 
+        if stage == 0:
+            prepare(0)
         traces = dot(jnp.concatenate(highs + lows, axis=0), pick_ref[...]).astype(half_type)
         columns = []
         for f in range(5):
@@ -420,6 +434,8 @@
             )
             kept = jnp.where(out_match, side, 0.0)
             own_rows.append(pair_rows(kept + swap_halves(kept), low_t))
+        if stage == 0:
+            prepare(2)
         coded = dot(jnp.concatenate(own_rows, axis=0), send_mat_ref[...])
 
         def choose(source, rows_at, rows, masks, first):
@@ -460,6 +476,10 @@
         ]
         rest_parts = [split(value * out_high_faces) for value in rest_fields]
 
+        if stage == 0:
+            prepare(4)
+            prepare(5)
+            prepare(6)
         grad = dot(
             jnp.concatenate([highs[1], highs[4], lows[1], lows[4]], axis=0), along_x_ref[:512]
         )
@@ -526,6 +546,9 @@
             turned = swap_halves(value)
             fields.append(pair_rows(jnp.where(low_b, value, turned), low_b))
             fields.append(pair_rows(jnp.where(low_b, turned, value), low_b))
+        if stage == 0:
+            prepare(3)
+            prepare(1)
         taken = dot(jnp.concatenate(fields, axis=0), take_mat_ref[...])
         chosen = [choose(taken, f * rows, rows, both_masks, 0) for f in range(4)]
 
@@ -585,6 +608,7 @@
             finished.append(result[f] + lift * (nodes + rim_nodes))
         return finished
 
+    loads[0].wait()
     current = [state_ref[f] for f in range(5)]
     change = rates(current, 0)
     current = [current[f] + change[f] for f in range(5)]
@@ -613,28 +637,8 @@
     elements = state.shape[1]
     half_rows = -(-cap_tile // 4) * 4
     sizes = (curves, tiles, elements, cap_tile, cap_curve, half_rows)
-    smem = pl.BlockSpec(memory_space=pltpu.SMEM)
-    vmem = pl.BlockSpec(memory_space=pltpu.VMEM)
     block = 2 * half_rows
-    return pl.pallas_call(
-        functools.partial(section_kernel, sizes),
-        out_shape=jax.ShapeDtypeStruct(state.shape, state.dtype),
-        in_specs=[vmem] + [smem] * 9 + [vmem] * 7,
-        out_specs=vmem,
-        scratch_shapes=[
-            pltpu.VMEM((3, tiles, block, 256), jnp.float32),
-            pltpu.VMEM((3, tiles, block, 256), jnp.float32),
-            pltpu.VMEM((3, 2, cap_curve, 256), jnp.float32),
-            pltpu.VMEM((3, 2, cap_curve, 256), jnp.float32),
-            pltpu.SemaphoreType.DMA((3, tiles)),
-            pltpu.SemaphoreType.DMA((3, tiles)),
-            pltpu.SemaphoreType.DMA((3, 2)),
-            pltpu.SemaphoreType.DMA((3, 2)),
-        ],
-        compiler_params=pltpu.CompilerParams(
-            collective_id=0, has_side_effects=True, vmem_limit_bytes=40 * 1024 * 1024
-        ),
-    )(
+    operands = [
         state,
         levels,
         send_faces,
@@ -646,7 +650,38 @@
         curve_orients,
         curve_counts,
         *tables(),
-    )
+    ]
+    held = [
+        pltpu.SMEM(value.shape, value.dtype)
+        if value.dtype == jnp.int32
+        else pltpu.VMEM(value.shape, value.dtype)
+        for value in operands
+    ]
+    return pl.pallas_call(
+        functools.partial(section_kernel, sizes),
+        out_shape=jax.ShapeDtypeStruct(state.shape, state.dtype),
+        in_specs=[pl.BlockSpec(memory_space=pl.ANY)] * operand_count,
+        out_specs=pl.BlockSpec(memory_space=pltpu.VMEM),
+        scratch_shapes=held
+        + [
+            pltpu.VMEM((3, tiles, block, 256), jnp.float32),
+            pltpu.VMEM((3, tiles, block, 256), jnp.float32),
+            pltpu.VMEM((3, 2, cap_curve, 256), jnp.float32),
+            pltpu.VMEM((3, 2, cap_curve, 256), jnp.float32),
+            pltpu.SemaphoreType.DMA((3, tiles)),
+            pltpu.SemaphoreType.DMA((3, tiles)),
+            pltpu.SemaphoreType.DMA((3, 2)),
+            pltpu.SemaphoreType.DMA((3, 2)),
+            pltpu.SemaphoreType.DMA((operand_count,)),
+        ]
+        + [
+            pltpu.VMEM((value.shape[0] * times, value.shape[1]), half_type)
+            for value, times in zip(operands[10:], (1, 1, 4, 4, 2, 2, 2))
+        ],
+        compiler_params=pltpu.CompilerParams(
+            collective_id=0, has_side_effects=True, vmem_limit_bytes=60 * 1024 * 1024
+        ),
+    )(*operands)
 
 
 def solution(mesh):

time: 33.5 us -> 20.4 us (0.61)
  local copies, waits for them, and re-layouts: 14.8 us -> 1.72 us
  Pallas kernels: 18.1 us -> 18.5 us
    unnamed x35 -> x1, local copies, waits for them, and re-layouts: 14.8 us -> 1.72 us
    pallas_call x1, Pallas kernels: 18.1 us -> 18.5 us  [shards(): pl.pallas_call(functools.partial(section_kernel, sizes), out_shape=jax.Sh...]
where the time goes in v2:
time: 20.4 us; the launch traced here: 20.2 us
  Pallas kernels  18.5 us (91%)
  local copies, waits for them, and re-layouts  1.72 us (8%)
    pallas_call x1, Pallas kernels, shards(): pl.pallas_call(functools.partial(section_kernel, sizes), out_shape=jax.Sh...  18.5 us
    unnamed x1, local copies, waits for them, and re-layouts  1.72 us

profile of v2, /device:TPU:0, one launch (start us, length us, event | category | flops | bytes accessed | tf_op | source)
XLA Modules:
  0.0 20.2 jit_solution(16694938188634695535)
XLA Ops:
  0.0 18.5 %shard_map.163 = f32[5,32,512]{2,1,0:T(8,128)} custom-call(f32[5,32,512]{2,1,0:T(8,128)} %refs_0_.1, s32[32]{0:T(128)} %refs_1_.1, s32[4,4]{1,0:T(4,128)} %refs_2_.1, s32[4]{0:T(128)} %refs_3_.1, s32[4,4]{1,0:T(4,128)} %refs_4_.1, s32[4,4]{1,0:T(4,128)} %refs_5_.1, s32[4]{0:T(128)} %refs_6_.1, s32[2,16]{1,0:T(2,128)} %refs_7_.1, s32[2,16]{1,0:T(2,128)} %refs_8_.1, ...), custom_call_target="tpu_custom_call" | custom-call | tf_op jit(solution)/shard_map/pallas_call | solution.py:660
  18.5 1.7 %copy.19 = f32[5,32,512]{2,1,0:T(8,128)} copy(f32[5,32,512]{2,1,0:T(8,128)} %shard_map.163) | data formatting | bytes 655360

commit v3 on v2

--- a/solution.py
+++ b/solution.py
@@ -133,6 +133,7 @@
         curve_send_sem,
         curve_recv_sem,
         load_sem,
+        held_state,
         *ready,
     ) = refs[2 * operand_count + 1 :]
     pick_ref, spread_ref, send_mat_ref, take_mat_ref, along_x_ref, along_y_ref, along_z_ref = ready
@@ -224,9 +225,10 @@
             blocks.append(value)
         return jnp.concatenate(blocks, axis=0)
 
-    def along_lanes(keys):
-        lane = lax.broadcasted_iota(jnp.int32, (8, len(keys)), 1)
-        value = jnp.full((8, len(keys)), -1, jnp.int32)
+    def along_lanes(keys, times):
+        count = len(keys)
+        lane = lax.broadcasted_iota(jnp.int32, (8, times * count), 1) % count
+        value = jnp.full((8, times * count), -1, jnp.int32)
         for at, key in enumerate(keys):
             value = jnp.where(lane == at, key, value)
         return jnp.concatenate([value] * (elements // 8), axis=0)
@@ -294,12 +296,14 @@
     in_part = lane_s < 2 * tile_rows
     first_half = (lane_s & (block - 1)) < half_rows
     lane_from_send = first_half != in_part
-    t_elem, t_face, _, _ = decode(along_lanes(in_keys * 2 + out_keys * 2), lane_from_send)
+    t_elem, t_face, _, _ = decode(
+        jnp.where(in_part, along_lanes(in_keys, 4), along_lanes(out_keys, 4)), lane_from_send
+    )
     t_hit = t_elem == lax.broadcasted_iota(jnp.int32, lane_shape, 0)
     tile_scatter = one_hot(t_hit)
     rim_shape = (elements, 2 * curve_rows)
     c_elem, c_face, _, _ = decode(
-        along_lanes(rim_keys * 2), lax.broadcasted_iota(jnp.int32, rim_shape, 1) < 0
+        along_lanes(rim_keys, 2), lax.broadcasted_iota(jnp.int32, rim_shape, 1) < 0
     )
     c_hit = c_elem == lax.broadcasted_iota(jnp.int32, rim_shape, 0)
     rim_scatter = one_hot(c_hit)
@@ -401,7 +405,9 @@
             [packed(sum_part, vel_part, low_c), packed(rim_vals[2], rim_vals[3], low_c)], axis=1
         )
         curve_out[stage] = rim_send.reshape(2, cap_curve, 256)
-        if stage == 0:
+
+        @pl.when(stage == 0)
+        def _():
             pl.semaphore_wait(
                 barrier, tiles - 1 + has_prev.astype(jnp.int32) + has_next.astype(jnp.int32)
             )
@@ -414,8 +420,10 @@
         def _():
             curve_copy(stage, 1).start()
 
-        if stage == 0:
+        @pl.when(stage == 0)
+        def _():
             prepare(0)
+
         traces = dot(jnp.concatenate(highs + lows, axis=0), pick_ref[...]).astype(half_type)
         columns = []
         for f in range(5):
@@ -434,8 +442,10 @@
             )
             kept = jnp.where(out_match, side, 0.0)
             own_rows.append(pair_rows(kept + swap_halves(kept), low_t))
-        if stage == 0:
+        @pl.when(stage == 0)
+        def _():
             prepare(2)
+
         coded = dot(jnp.concatenate(own_rows, axis=0), send_mat_ref[...])
 
         def choose(source, rows_at, rows, masks, first):
@@ -476,10 +486,12 @@
         ]
         rest_parts = [split(value * out_high_faces) for value in rest_fields]
 
-        if stage == 0:
+        @pl.when(stage == 0)
+        def _():
             prepare(4)
             prepare(5)
             prepare(6)
+
         grad = dot(
             jnp.concatenate([highs[1], highs[4], lows[1], lows[4]], axis=0), along_x_ref[:512]
         )
@@ -546,9 +558,11 @@
             turned = swap_halves(value)
             fields.append(pair_rows(jnp.where(low_b, value, turned), low_b))
             fields.append(pair_rows(jnp.where(low_b, turned, value), low_b))
-        if stage == 0:
+        @pl.when(stage == 0)
+        def _():
             prepare(3)
             prepare(1)
+
         taken = dot(jnp.concatenate(fields, axis=0), take_mat_ref[...])
         chosen = [choose(taken, f * rows, rows, both_masks, 0) for f in range(4)]
 
@@ -609,14 +623,19 @@
         return finished
 
     loads[0].wait()
-    current = [state_ref[f] for f in range(5)]
-    change = rates(current, 0)
-    current = [current[f] + change[f] for f in range(5)]
-    change = rates(current, 1)
-    current = [0.75 * state_ref[f] + 0.25 * (current[f] + change[f]) for f in range(5)]
-    change = rates(current, 2)
-    for f in range(5):
-        out_ref[f] = state_ref[f] / 3.0 + (2.0 / 3.0) * (current[f] + change[f])
+    held_state[...] = state_ref[...]
+
+    def section(stage, carry):
+        current = [held_state[f] for f in range(5)]
+        change = rates(current, stage)
+        keep = jnp.where(stage == 0, 0.0, jnp.where(stage == 1, 0.75, 1.0 / 3.0))
+        move = jnp.where(stage == 0, 1.0, jnp.where(stage == 1, 0.25, 2.0 / 3.0))
+        for f in range(5):
+            held_state[f] = keep * state_ref[f] + move * (held_state[f] + change[f])
+        return carry
+
+    lax.fori_loop(0, 3, section, 0)
+    out_ref[...] = held_state[...]
 
 
 def shards(
@@ -673,6 +692,7 @@
             pltpu.SemaphoreType.DMA((3, 2)),
             pltpu.SemaphoreType.DMA((3, 2)),
             pltpu.SemaphoreType.DMA((operand_count,)),
+            pltpu.VMEM(state.shape, jnp.float32),
         ]
         + [
             pltpu.VMEM((value.shape[0] * times, value.shape[1]), half_type)

time: 20.4 us -> 20.9 us (1.025)
  Pallas kernels: 18.5 us -> 19 us
    pallas_call x1, Pallas kernels: 18.5 us -> 19 us  [shards(): pl.pallas_call(functools.partial(section_kernel, sizes), out_shape=jax.Sh...]
where the time goes in v3:
time: 20.9 us; the launch traced here: 20.7 us
  Pallas kernels  19 us (91%)
  local copies, waits for them, and re-layouts  1.72 us (8%)
    pallas_call x1, Pallas kernels, shards(): pl.pallas_call(functools.partial(section_kernel, sizes), out_shape=jax.Sh...  19 us
    unnamed x1, local copies, waits for them, and re-layouts  1.72 us

profile of v3, /device:TPU:0, one launch (start us, length us, event | category | flops | bytes accessed | tf_op | source)
XLA Modules:
  0.0 20.7 jit_solution(799219575591681688)
XLA Ops:
  0.0 19.0 %shard_map.163 = f32[5,32,512]{2,1,0:T(8,128)} custom-call(f32[5,32,512]{2,1,0:T(8,128)} %refs_0_.1, s32[32]{0:T(128)} %refs_1_.1, s32[4,4]{1,0:T(4,128)} %refs_2_.1, s32[4]{0:T(128)} %refs_3_.1, s32[4,4]{1,0:T(4,128)} %refs_4_.1, s32[4,4]{1,0:T(4,128)} %refs_5_.1, s32[4]{0:T(128)} %refs_6_.1, s32[2,16]{1,0:T(2,128)} %refs_7_.1, s32[2,16]{1,0:T(2,128)} %refs_8_.1, ...), custom_call_target="tpu_custom_call" | custom-call | tf_op jit(solution)/shard_map/pallas_call | solution.py:679
  19.0 1.7 %copy.19 = f32[5,32,512]{2,1,0:T(8,128)} copy(f32[5,32,512]{2,1,0:T(8,128)} %shard_map.163) | data formatting | bytes 655360

commit v4 on v3

--- a/solution.py
+++ b/solution.py
@@ -190,48 +190,53 @@
     for at in range(1, 10):
         loads[at].wait()
 
-    def send_key(peer, slot):
-        if slot >= cap_tile:
-            return jnp.int32(-1)
-        return jnp.where(slot < send_counts_ref[peer], send_faces_ref[peer, slot] * 16, -1)
-
-    def recv_key(peer, slot):
-        if slot >= cap_tile:
-            return jnp.int32(-1)
-        value = recv_faces_ref[peer, slot] * 16 + recv_orients_ref[peer, slot]
-        return jnp.where(slot < recv_counts_ref[peer], value, -1)
-
-    def curve_key(side, slot):
-        value = curve_faces_ref[side, slot] * 16 + curve_orients_ref[side, slot]
-        return jnp.where(slot < curve_counts_ref[side], value, -1)
-
-    out_keys = []
-    in_keys = []
-    for off in range(tiles):
-        out_keys += [send_key(to_peer[off], slot) for slot in range(half_rows)]
-        out_keys += [recv_key(to_peer[off], slot) for slot in range(half_rows)]
-        in_keys += [recv_key(from_peer[off], slot) for slot in range(half_rows)]
-        in_keys += [send_key(from_peer[off], slot) for slot in range(half_rows)]
-    rim_keys = [curve_key(side, slot) for side in range(2) for slot in range(cap_curve)]
+    def spread_down(live_rows, rows):
+        column = jnp.sum(live_rows.astype(jnp.float32), axis=1, keepdims=True)
+        return jnp.broadcast_to(column - 1.0, (rows, 128))
+
+    tile_lane = lax.broadcasted_iota(jnp.int32, (block, cap_tile), 1)
+    tile_sub = lax.broadcasted_iota(jnp.int32, (block, cap_tile), 0)
+    tile_first = tile_sub < half_rows
+    tile_own = tile_lane == (tile_sub & (half_rows - 1))
+
+    def tile_key_rows(peer, send_first):
+        row = pl.ds(peer, 1)
+        sent = send_faces_ref[row, :] * 16 + 1
+        got = recv_faces_ref[row, :] * 16 + recv_orients_ref[row, :] + 1
+        row_lane = lax.broadcasted_iota(jnp.int32, (1, cap_tile), 1)
+        sent = jnp.where(row_lane < send_counts_ref[peer], sent, 0)
+        got = jnp.where(row_lane < recv_counts_ref[peer], got, 0)
+        pair = (sent, got) if send_first else (got, sent)
+        both = jnp.where(tile_first, pair[0], pair[1])
+        return spread_down(jnp.where(tile_own, both, 0), block)
+
+    def curve_key_rows(side):
+        shape = (cap_curve, cap_curve)
+        lane = lax.broadcasted_iota(jnp.int32, shape, 1)
+        sub = lax.broadcasted_iota(jnp.int32, shape, 0)
+        row = curve_faces_ref[side : side + 1, :] * 16 + curve_orients_ref[side : side + 1, :] + 1
+        own = jnp.logical_and(lane == sub, lane < curve_counts_ref[side])
+        return spread_down(jnp.where(own, row, 0), cap_curve)
+
+    out_keys = jnp.concatenate([tile_key_rows(p, True) for p in to_peer], axis=0)
+    in_keys = jnp.concatenate([tile_key_rows(p, False) for p in from_peer], axis=0)
+    rim_keys = jnp.concatenate([curve_key_rows(side) for side in range(2)], axis=0)
 
     sub_iota = lax.broadcasted_iota(jnp.int32, (8, 128), 0)
 
     def down_rows(keys):
-        blocks = []
-        for start in range(0, len(keys), 8):
-            value = jnp.full((8, 128), -1, jnp.int32)
-            for at in range(8):
-                value = jnp.where(sub_iota == at, keys[start + at], value)
-            blocks.append(value)
-        return jnp.concatenate(blocks, axis=0)
+        return keys.astype(jnp.int32)
 
     def along_lanes(keys, times):
-        count = len(keys)
-        lane = lax.broadcasted_iota(jnp.int32, (8, times * count), 1) % count
-        value = jnp.full((8, times * count), -1, jnp.int32)
-        for at, key in enumerate(keys):
-            value = jnp.where(lane == at, key, value)
-        return jnp.concatenate([value] * (elements // 8), axis=0)
+        count = keys.shape[0]
+        width = times * count
+        shape = (count, width)
+        own = lax.broadcasted_iota(jnp.int32, shape, 1) % count == lax.broadcasted_iota(
+            jnp.int32, shape, 0
+        )
+        wide = jnp.concatenate([keys] * (-(-width // 128)), axis=1)[:, :width]
+        value = jnp.sum(jnp.where(own, wide, 0.0), axis=0, keepdims=True)
+        return jnp.broadcast_to(value, (elements, width)).astype(jnp.int32)
 
     def decode(keys, from_send):
         live = keys >= 0
@@ -391,10 +396,14 @@
         highs = [part[0] for part in parts]
         lows = [part[1] for part in parts]
 
+        if stage == 0:
+            prepare(0)
+            prepare(2)
         low_e = lax.broadcasted_iota(jnp.int32, (elements, 128), 1) < 64
         ends = [split(jnp.where(low_e, v[:, :128], v[:, 384:])) for v in current]
         ends = jnp.concatenate([jnp.concatenate(e, axis=0) for e in ends], axis=1)
         rim = dot(rim_gather, ends)
+        traces = dot(jnp.concatenate(highs + lows, axis=0), pick_ref[...]).astype(half_type)
         rim_vals = []
         for f in range(5):
             kept = jnp.where(rim_match, rim[:, 128 * f : 128 * f + 128], 0.0)
@@ -405,9 +414,7 @@
             [packed(sum_part, vel_part, low_c), packed(rim_vals[2], rim_vals[3], low_c)], axis=1
         )
         curve_out[stage] = rim_send.reshape(2, cap_curve, 256)
-
-        @pl.when(stage == 0)
-        def _():
+        if stage == 0:
             pl.semaphore_wait(
                 barrier, tiles - 1 + has_prev.astype(jnp.int32) + has_next.astype(jnp.int32)
             )
@@ -420,11 +427,6 @@
         def _():
             curve_copy(stage, 1).start()
 
-        @pl.when(stage == 0)
-        def _():
-            prepare(0)
-
-        traces = dot(jnp.concatenate(highs + lows, axis=0), pick_ref[...]).astype(half_type)
         columns = []
         for f in range(5):
             at = f * elements
@@ -442,10 +444,6 @@
             )
             kept = jnp.where(out_match, side, 0.0)
             own_rows.append(pair_rows(kept + swap_halves(kept), low_t))
-        @pl.when(stage == 0)
-        def _():
-            prepare(2)
-
         coded = dot(jnp.concatenate(own_rows, axis=0), send_mat_ref[...])
 
         def choose(source, rows_at, rows, masks, first):
@@ -486,12 +484,10 @@
         ]
         rest_parts = [split(value * out_high_faces) for value in rest_fields]
 
-        @pl.when(stage == 0)
-        def _():
+        if stage == 0:
             prepare(4)
             prepare(5)
             prepare(6)
-
         grad = dot(
             jnp.concatenate([highs[1], highs[4], lows[1], lows[4]], axis=0), along_x_ref[:512]
         )
@@ -528,20 +524,20 @@
             )
         result.append(to_sum - total_damp * current[4])
 
-        for copy in copies:
-            copy.wait()
+        if stage == 0:
+            prepare(3)
+            prepare(1)
 
         @pl.when(has_prev)
         def _():
-            copy = curve_copy(stage, 0)
-            copy.wait_send()
             curve_copy(stage, 1).wait_recv()
 
         @pl.when(has_next)
         def _():
-            copy = curve_copy(stage, 1)
-            copy.wait_send()
             curve_copy(stage, 0).wait_recv()
+
+        for copy in copies:
+            copy.wait_recv()
 
         arrived = jnp.concatenate(
             [
@@ -558,11 +554,6 @@
             turned = swap_halves(value)
             fields.append(pair_rows(jnp.where(low_b, value, turned), low_b))
             fields.append(pair_rows(jnp.where(low_b, turned, value), low_b))
-        @pl.when(stage == 0)
-        def _():
-            prepare(3)
-            prepare(1)
-
         taken = dot(jnp.concatenate(fields, axis=0), take_mat_ref[...])
         chosen = [choose(taken, f * rows, rows, both_masks, 0) for f in range(4)]
 
@@ -625,17 +616,30 @@
     loads[0].wait()
     held_state[...] = state_ref[...]
 
-    def section(stage, carry):
+    for stage in range(3):
         current = [held_state[f] for f in range(5)]
         change = rates(current, stage)
-        keep = jnp.where(stage == 0, 0.0, jnp.where(stage == 1, 0.75, 1.0 / 3.0))
-        move = jnp.where(stage == 0, 1.0, jnp.where(stage == 1, 0.25, 2.0 / 3.0))
         for f in range(5):
-            held_state[f] = keep * state_ref[f] + move * (held_state[f] + change[f])
-        return carry
-
-    lax.fori_loop(0, 3, section, 0)
-    out_ref[...] = held_state[...]
+            moved = held_state[f] + change[f]
+            if stage == 0:
+                held_state[f] = moved
+            elif stage == 1:
+                held_state[f] = 0.75 * state_ref[f] + 0.25 * moved
+            else:
+                out_ref[f] = state_ref[f] / 3.0 + (2.0 / 3.0) * moved
+    for stage in range(3):
+        for copy in tile_copies(stage):
+            copy.wait_send()
+
+    @pl.when(has_prev)
+    def _():
+        for stage in range(3):
+            curve_copy(stage, 0).wait_send()
+
+    @pl.when(has_next)
+    def _():
+        for stage in range(3):
+            curve_copy(stage, 1).wait_send()
 
 
 def shards(
@@ -672,13 +676,13 @@
     ]
     held = [
         pltpu.SMEM(value.shape, value.dtype)
-        if value.dtype == jnp.int32
+        if value.ndim == 1
         else pltpu.VMEM(value.shape, value.dtype)
         for value in operands
     ]
     return pl.pallas_call(
         functools.partial(section_kernel, sizes),
-        out_shape=jax.ShapeDtypeStruct(state.shape, state.dtype),
+        out_shape=pltpu.VMEM(state.shape, state.dtype),
         in_specs=[pl.BlockSpec(memory_space=pl.ANY)] * operand_count,
         out_specs=pl.BlockSpec(memory_space=pltpu.VMEM),
         scratch_shapes=held

time: 20.9 us -> 18.1 us (0.87)
  Pallas kernels: 19 us -> 17.2 us
  local copies, waits for them, and re-layouts: 1.72 us -> 0.73 us
    pallas_call x1, Pallas kernels: 19 us -> 17.2 us  [shards(): pl.pallas_call(functools.partial(section_kernel, sizes), out_shape=pltpu....]
    unnamed x1, local copies, waits for them, and re-layouts: 1.72 us -> 0.73 us
where the time goes in v4:
time: 18.1 us; the launch traced here: 18 us
  Pallas kernels  17.2 us (95%)
  local copies, waits for them, and re-layouts  0.73 us (4%)
    pallas_call x1, Pallas kernels, shards(): pl.pallas_call(functools.partial(section_kernel, sizes), out_shape=pltpu....  17.2 us
    unnamed x1, local copies, waits for them, and re-layouts  0.73 us

profile of v4, /device:TPU:0, one launch (start us, length us, event | category | flops | bytes accessed | tf_op | source)
XLA Modules:
  0.0 18.0 jit_solution(7301173724088095142)
XLA Ops:
  0.0 17.2 %shard_map.163 = f32[5,32,512]{2,1,0:T(8,128)S(1)} custom-call(f32[5,32,512]{2,1,0:T(8,128)} %refs_0_.1, s32[32]{0:T(128)} %refs_1_.1, s32[4,4]{1,0:T(4,128)} %refs_2_.1, s32[4]{0:T(128)} %refs_3_.1, s32[4,4]{1,0:T(4,128)} %refs_4_.1, s32[4,4]{1,0:T(4,128)} %refs_5_.1, s32[4]{0:T(128)} %refs_6_.1, s32[2,16]{1,0:T(2,128)} %refs_7_.1, s32[2,16]{1,0:T(2,128)} %refs_8_.1, ...), custom_call_target="tpu_custom_call" | custom-call | tf_op jit(solution)/shard_map/pallas_call | solution.py:683
  17.2 0.7 %copy.19 = f32[5,32,512]{2,1,0:T(8,128)} copy(f32[5,32,512]{2,1,0:T(8,128)S(1)} %shard_map.163) | data formatting | bytes 655360

commit v5 on v4

--- a/solution.py
+++ b/solution.py
@@ -13,7 +13,7 @@
 half_type = jnp.bfloat16
 MESH = pl.DeviceIdType.MESH
 operand_count = 17
-load_order = [3, 2, 5, 4, 6, 8, 7, 9, 1, 0, 10, 12, 14, 15, 16, 13, 11]
+load_order = [0, 2, 4, 5, 3, 6, 7, 8, 9, 1, 10, 12, 14, 15, 16, 13, 11]
 inner_nodes = [
     -0.8717401485096066,
     -0.5917001814331423,
@@ -81,16 +81,25 @@
             pick[64 * s + 8 * t, 64 + column] = 1.0
             pick[64 * s + 56 + t, 128 + column] = 1.0
             pick[64 * s + 8 * t + 7, 192 + column] = 1.0
+    def parts(matrix):
+        high = matrix.astype(ml_dtypes.bfloat16)
+        low = (matrix - high.astype(np.float64)).astype(ml_dtypes.bfloat16)
+        return high, low
+
+    def stacked(mats):
+        high, low = parts(np.concatenate([m.T for m in mats], axis=1))
+        return np.concatenate([high, high, low, np.zeros_like(low)], axis=0)
+
     return [
-        jnp.asarray(m.astype(np.float32))
+        jnp.asarray(m.astype(ml_dtypes.bfloat16))
         for m in (
             pick,
             pick.T,
-            np.concatenate([m.T for m in send], axis=1),
-            np.concatenate([m.T for m in take], axis=1),
-            np.kron(deriv.T, np.eye(64)),
-            np.kron(np.eye(4), np.kron(deriv.T, np.eye(8))),
-            np.kron(np.eye(32), deriv.T),
+            stacked(send),
+            stacked(take),
+            np.concatenate(parts(np.kron(deriv.T, np.eye(64))), axis=0),
+            np.concatenate(parts(np.kron(np.eye(4), np.kron(deriv.T, np.eye(8)))), axis=0),
+            np.concatenate(parts(np.kron(np.eye(32), deriv.T)), axis=0),
         )
     ]
 
@@ -134,9 +143,7 @@
         curve_recv_sem,
         load_sem,
         held_state,
-        *ready,
     ) = refs[2 * operand_count + 1 :]
-    pick_ref, spread_ref, send_mat_ref, take_mat_ref, along_x_ref, along_y_ref, along_z_ref = ready
     (
         state_ref,
         levels_ref,
@@ -148,7 +155,13 @@
         curve_faces_ref,
         curve_orients_ref,
         curve_counts_ref,
-        *wide,
+        pick_ref,
+        spread_ref,
+        send_mat_ref,
+        take_mat_ref,
+        along_x_ref,
+        along_y_ref,
+        along_z_ref,
     ) = held
     loads = [
         pltpu.make_async_copy(source, target, load_sem.at[at])
@@ -283,9 +296,9 @@
     rim_first = rim_row < cap_curve
     rim_match = low_c == rim_first
     rim_sign = jnp.where(rim_first, 1.0, -1.0)
-    both_codes = jnp.concatenate([in_code, rim_turn], axis=0)
-    upper_b = jnp.where(lax.broadcasted_iota(jnp.int32, both_codes.shape, 1) < 64, 0, 1)
-    both_masks = [jnp.where(both_codes == 2 * j + upper_b, 1.0, 0.0) for j in range(7)]
+    upper_c = jnp.where(low_c, 0, 1)
+    in_masks = [jnp.where(in_code == 2 * j + upper_t, 1.0, 0.0) for j in range(7)]
+    rim_masks = [jnp.where(rim_turn == 2 * j + upper_c, 1.0, 0.0) for j in range(4)]
     rim_place = jnp.where(rim_match, 1.0, 0.0)
 
     def one_hot(flags):
@@ -350,17 +363,6 @@
     total_damp = side_damp[0] + side_damp[1] + side_damp[2]
     vel_damp = [own_damp[d] + (total_damp - side_damp[d]) for d in range(3)]
 
-    def prepare(at):
-        loads[10 + at].wait()
-        value = wide[at][...]
-        high, low = split(value)
-        if at < 2:
-            ready[at][...] = high
-        elif at < 4:
-            ready[at][...] = jnp.concatenate([high, high, low, jnp.zeros_like(low)], axis=0)
-        else:
-            ready[at][...] = jnp.concatenate([high, low], axis=0)
-
     def tile_copies(stage):
         return [
             pltpu.make_async_remote_copy(
@@ -397,8 +399,8 @@
         lows = [part[1] for part in parts]
 
         if stage == 0:
-            prepare(0)
-            prepare(2)
+            loads[10].wait()
+            loads[12].wait()
         low_e = lax.broadcasted_iota(jnp.int32, (elements, 128), 1) < 64
         ends = [split(jnp.where(low_e, v[:, :128], v[:, 384:])) for v in current]
         ends = jnp.concatenate([jnp.concatenate(e, axis=0) for e in ends], axis=1)
@@ -485,9 +487,9 @@
         rest_parts = [split(value * out_high_faces) for value in rest_fields]
 
         if stage == 0:
-            prepare(4)
-            prepare(5)
-            prepare(6)
+            loads[14].wait()
+            loads[15].wait()
+            loads[16].wait()
         grad = dot(
             jnp.concatenate([highs[1], highs[4], lows[1], lows[4]], axis=0), along_x_ref[:512]
         )
@@ -525,8 +527,18 @@
         result.append(to_sum - total_damp * current[4])
 
         if stage == 0:
-            prepare(3)
-            prepare(1)
+            loads[13].wait()
+            loads[11].wait()
+
+        def take(arrived, rows, low, masks):
+            fields = []
+            for at in range(2):
+                value = arrived[:, 128 * at : 128 * at + 128]
+                turned = swap_halves(value)
+                fields.append(pair_rows(jnp.where(low, value, turned), low))
+                fields.append(pair_rows(jnp.where(low, turned, value), low))
+            taken = dot(jnp.concatenate(fields, axis=0), take_mat_ref[:, : 128 * len(masks)])
+            return [choose(taken, f * rows, rows, masks, 0) for f in range(4)]
 
         @pl.when(has_prev)
         def _():
@@ -536,29 +548,8 @@
         def _():
             curve_copy(stage, 0).wait_recv()
 
-        for copy in copies:
-            copy.wait_recv()
-
-        arrived = jnp.concatenate(
-            [
-                tile_in[stage].reshape(tile_rows, 256),
-                curve_in[stage].reshape(curve_rows, 256),
-            ],
-            axis=0,
-        )
-        rows = tile_rows + curve_rows
-        low_b = lax.broadcasted_iota(jnp.int32, (rows, 128), 1) < 64
-        fields = []
-        for at in range(2):
-            value = arrived[:, 128 * at : 128 * at + 128]
-            turned = swap_halves(value)
-            fields.append(pair_rows(jnp.where(low_b, value, turned), low_b))
-            fields.append(pair_rows(jnp.where(low_b, turned, value), low_b))
-        taken = dot(jnp.concatenate(fields, axis=0), take_mat_ref[...])
-        chosen = [choose(taken, f * rows, rows, both_masks, 0) for f in range(4)]
-
-        rim_in = [value[tile_rows:] * rim_place for value in chosen]
-        rim_cols = [jnp.concatenate(split(value), axis=0) for value in rim_in]
+        rim_vals = take(curve_in[stage].reshape(curve_rows, 256), curve_rows, low_c, rim_masks)
+        rim_cols = [jnp.concatenate(split(value * rim_place), axis=0) for value in rim_vals]
         placed = dot(rim_scatter, jnp.concatenate(rim_cols, axis=1))
         place_sum = -0.5 * placed[:, :128]
         place_vel = -0.5 * placed[:, 128:256]
@@ -570,8 +561,21 @@
             0.5 * placed[:, 384:512],
             place_pres,
         ]
-
-        tile_vals = [value[:tile_rows] for value in chosen]
+        for f in range(5):
+            rim_nodes = jnp.concatenate(
+                [
+                    jnp.where(low_e, rim_fields[f], 0.0),
+                    jnp.zeros((elements, 256), jnp.float32),
+                    jnp.where(low_e, 0.0, rim_fields[f]),
+                ],
+                axis=1,
+            )
+            result[f] = result[f] + lift * rim_nodes
+
+        for copy in copies:
+            copy.wait_recv()
+        tile_vals = take(tile_in[stage].reshape(tile_rows, 256), tile_rows, low_t, in_masks)
+
         put_sum = -0.5 * tile_vals[0]
         put_n = -0.5 * tile_vals[1]
         put_o = 0.5 * tile_vals[3]
@@ -597,20 +601,11 @@
             spread_ref[...],
         )
         finished = []
-        zero_middle = jnp.zeros((elements, 256), jnp.float32)
         for f in range(5):
             at = f * elements
             low_at = (5 + f) * elements
             nodes = spread[at : at + elements] + spread[low_at : low_at + elements]
-            rim_nodes = jnp.concatenate(
-                [
-                    jnp.where(low_e, rim_fields[f], 0.0),
-                    zero_middle,
-                    jnp.where(low_e, 0.0, rim_fields[f]),
-                ],
-                axis=1,
-            )
-            finished.append(result[f] + lift * (nodes + rim_nodes))
+            finished.append(result[f] + lift * nodes)
         return finished
 
     loads[0].wait()
@@ -697,10 +692,6 @@
             pltpu.SemaphoreType.DMA((3, 2)),
             pltpu.SemaphoreType.DMA((operand_count,)),
             pltpu.VMEM(state.shape, jnp.float32),
-        ]
-        + [
-            pltpu.VMEM((value.shape[0] * times, value.shape[1]), half_type)
-            for value, times in zip(operands[10:], (1, 1, 4, 4, 2, 2, 2))
         ],
         compiler_params=pltpu.CompilerParams(
             collective_id=0, has_side_effects=True, vmem_limit_bytes=60 * 1024 * 1024

time: 18.1 us -> 18.4 us (1.017)
  Pallas kernels: 17.2 us -> 17.5 us
    pallas_call x1, Pallas kernels: 17.2 us -> 17.5 us  [shards(): pl.pallas_call(functools.partial(section_kernel, sizes), out_shape=pltpu....]
where the time goes in v5:
time: 18.4 us; the launch traced here: 18.3 us
  Pallas kernels  17.5 us (95%)
  local copies, waits for them, and re-layouts  0.73 us (4%)
    pallas_call x1, Pallas kernels, shards(): pl.pallas_call(functools.partial(section_kernel, sizes), out_shape=pltpu....  17.5 us
    unnamed x1, local copies, waits for them, and re-layouts  0.73 us

profile of v5, /device:TPU:0, one launch (start us, length us, event | category | flops | bytes accessed | tf_op | source)
XLA Modules:
  0.0 18.3 jit_solution(2259879483094227578)
XLA Ops:
  0.0 17.5 %shard_map.163 = f32[5,32,512]{2,1,0:T(8,128)S(1)} custom-call(f32[5,32,512]{2,1,0:T(8,128)} %refs_0_.1, s32[32]{0:T(128)} %refs_1_.1, s32[4,4]{1,0:T(4,128)} %refs_2_.1, s32[4]{0:T(128)} %refs_3_.1, s32[4,4]{1,0:T(4,128)} %refs_4_.1, s32[4,4]{1,0:T(4,128)} %refs_5_.1, s32[4]{0:T(128)} %refs_6_.1, s32[2,16]{1,0:T(2,128)} %refs_7_.1, s32[2,16]{1,0:T(2,128)} %refs_8_.1, ...), custom_call_target="tpu_custom_call" | custom-call | tf_op jit(solution)/shard_map/pallas_call | solution.py:678
  17.5 0.7 %copy.19 = f32[5,32,512]{2,1,0:T(8,128)} copy(f32[5,32,512]{2,1,0:T(8,128)S(1)} %shard_map.163) | data formatting | bytes 655360

commit v6 on v5

--- a/solution.py
+++ b/solution.py
@@ -95,7 +95,7 @@
         for m in (
             pick,
             pick.T,
-            stacked(send),
+            np.concatenate(parts(np.concatenate([m.T for m in send], axis=1)), axis=0),
             stacked(take),
             np.concatenate(parts(np.kron(deriv.T, np.eye(64))), axis=0),
             np.concatenate(parts(np.kron(np.eye(4), np.kron(deriv.T, np.eye(8)))), axis=0),
@@ -304,8 +304,8 @@
     def one_hot(flags):
         return jnp.where(flags, 1.0, 0.0).astype(half_type)
 
-    gather_lane = lax.broadcasted_iota(jnp.int32, (tile_rows, 2 * elements), 1) % elements
-    out_gather = one_hot(gather_lane == out_elem[:, : 2 * elements])
+    gather_lane = lax.broadcasted_iota(jnp.int32, (tile_rows, elements), 1)
+    out_gather = one_hot(gather_lane == out_elem[:, :elements])
     rim_lane = lax.broadcasted_iota(jnp.int32, (curve_rows, 2 * elements), 1) % elements
     rim_gather = one_hot(rim_lane == rim_elem[:, : 2 * elements])
 
@@ -405,7 +405,7 @@
         ends = [split(jnp.where(low_e, v[:, :128], v[:, 384:])) for v in current]
         ends = jnp.concatenate([jnp.concatenate(e, axis=0) for e in ends], axis=1)
         rim = dot(rim_gather, ends)
-        traces = dot(jnp.concatenate(highs + lows, axis=0), pick_ref[...]).astype(half_type)
+        traces = dot(jnp.concatenate(highs, axis=0), pick_ref[...]).astype(half_type)
         rim_vals = []
         for f in range(5):
             kept = jnp.where(rim_match, rim[:, 128 * f : 128 * f + 128], 0.0)
@@ -429,15 +429,7 @@
         def _():
             curve_copy(stage, 1).start()
 
-        columns = []
-        for f in range(5):
-            at = f * elements
-            low_at = (5 + f) * elements
-            columns.append(
-                jnp.concatenate(
-                    [traces[at : at + elements], traces[low_at : low_at + elements]], axis=0
-                )
-            )
+        columns = [traces[f * elements : (f + 1) * elements] for f in range(5)]
         own = dot(out_gather, jnp.concatenate(columns, axis=1))
         own_rows = []
         for f in range(5):
@@ -445,7 +437,7 @@
                 out_is_send, own[:, 256 * f + 128 : 256 * f + 256], own[:, 256 * f : 256 * f + 128]
             )
             kept = jnp.where(out_match, side, 0.0)
-            own_rows.append(pair_rows(kept + swap_halves(kept), low_t))
+            own_rows.append((kept + swap_halves(kept)).astype(half_type))
         coded = dot(jnp.concatenate(own_rows, axis=0), send_mat_ref[...])
 
         def choose(source, rows_at, rows, masks, first):
@@ -530,16 +522,6 @@
             loads[13].wait()
             loads[11].wait()
 
-        def take(arrived, rows, low, masks):
-            fields = []
-            for at in range(2):
-                value = arrived[:, 128 * at : 128 * at + 128]
-                turned = swap_halves(value)
-                fields.append(pair_rows(jnp.where(low, value, turned), low))
-                fields.append(pair_rows(jnp.where(low, turned, value), low))
-            taken = dot(jnp.concatenate(fields, axis=0), take_mat_ref[:, : 128 * len(masks)])
-            return [choose(taken, f * rows, rows, masks, 0) for f in range(4)]
-
         @pl.when(has_prev)
         def _():
             curve_copy(stage, 1).wait_recv()
@@ -548,7 +530,33 @@
         def _():
             curve_copy(stage, 0).wait_recv()
 
-        rim_vals = take(curve_in[stage].reshape(curve_rows, 256), curve_rows, low_c, rim_masks)
+        for copy in copies:
+            copy.wait_recv()
+
+        fields = []
+        for at in range(2):
+            span = slice(128 * at, 128 * at + 128)
+            for source, rows, low in (
+                (tile_in[stage], tile_rows, low_t),
+                (curve_in[stage], curve_rows, low_c),
+            ):
+                value = source.reshape(rows, 256)[:, span]
+                turned = swap_halves(value)
+                fields.append(
+                    (
+                        pair_rows(jnp.where(low, value, turned), low),
+                        pair_rows(jnp.where(low, turned, value), low),
+                    )
+                )
+        stacked = [fields[0][0], fields[0][1], fields[2][0], fields[2][1]]
+        stacked += [fields[1][0], fields[1][1], fields[3][0], fields[3][1]]
+        taken = dot(jnp.concatenate(stacked, axis=0), take_mat_ref[...])
+        tile_vals = [choose(taken, f * tile_rows, tile_rows, in_masks, 0) for f in range(4)]
+        rim_at = 4 * tile_rows
+        rim_vals = [
+            choose(taken, rim_at + f * curve_rows, curve_rows, rim_masks, 0) for f in range(4)
+        ]
+
         rim_cols = [jnp.concatenate(split(value * rim_place), axis=0) for value in rim_vals]
         placed = dot(rim_scatter, jnp.concatenate(rim_cols, axis=1))
         place_sum = -0.5 * placed[:, :128]
@@ -561,20 +569,6 @@
             0.5 * placed[:, 384:512],
             place_pres,
         ]
-        for f in range(5):
-            rim_nodes = jnp.concatenate(
-                [
-                    jnp.where(low_e, rim_fields[f], 0.0),
-                    jnp.zeros((elements, 256), jnp.float32),
-                    jnp.where(low_e, 0.0, rim_fields[f]),
-                ],
-                axis=1,
-            )
-            result[f] = result[f] + lift * rim_nodes
-
-        for copy in copies:
-            copy.wait_recv()
-        tile_vals = take(tile_in[stage].reshape(tile_rows, 256), tile_rows, low_t, in_masks)
 
         put_sum = -0.5 * tile_vals[0]
         put_n = -0.5 * tile_vals[1]
@@ -595,16 +589,18 @@
             columns.append(jnp.concatenate([first[0], first[1], zero_part, zero_part], axis=0))
             columns.append(jnp.concatenate([second[0], second[1], high, low], axis=0))
         on_faces = dot(tile_scatter, jnp.concatenate(columns, axis=1))
-        face_parts = [split(on_faces[:, 256 * f : 256 * f + 256]) for f in range(5)]
         spread = dot(
-            jnp.concatenate([p[0] for p in face_parts] + [p[1] for p in face_parts], axis=0),
+            jnp.concatenate(
+                [on_faces[:, 256 * f : 256 * f + 256].astype(half_type) for f in range(5)], axis=0
+            ),
             spread_ref[...],
         )
         finished = []
         for f in range(5):
-            at = f * elements
-            low_at = (5 + f) * elements
-            nodes = spread[at : at + elements] + spread[low_at : low_at + elements]
+            nodes = spread[f * elements : (f + 1) * elements]
+            first = nodes[:, :128] + jnp.where(low_e, rim_fields[f], 0.0)
+            last = nodes[:, 384:] + jnp.where(low_e, 0.0, rim_fields[f])
+            nodes = jnp.concatenate([first, nodes[:, 128:384], last], axis=1)
             finished.append(result[f] + lift * nodes)
         return finished
 

time: 18.4 us -> 17.4 us (0.946)
  Pallas kernels: 17.5 us -> 16.5 us
    pallas_call x1, Pallas kernels: 17.5 us -> 16.5 us  [shards(): pl.pallas_call(functools.partial(section_kernel, sizes), out_shape=pltpu....]
where the time goes in v6:
time: 17.4 us; the launch traced here: 17.2 us
  Pallas kernels  16.5 us (95%)
  local copies, waits for them, and re-layouts  0.73 us (4%)
    pallas_call x1, Pallas kernels, shards(): pl.pallas_call(functools.partial(section_kernel, sizes), out_shape=pltpu....  16.5 us
    unnamed x1, local copies, waits for them, and re-layouts  0.73 us

profile of v6, /device:TPU:0, one launch (start us, length us, event | category | flops | bytes accessed | tf_op | source)
XLA Modules:
  0.0 17.2 jit_solution(5185043606931508487)
XLA Ops:
  0.0 16.5 %shard_map.163 = f32[5,32,512]{2,1,0:T(8,128)S(1)} custom-call(f32[5,32,512]{2,1,0:T(8,128)} %refs_0_.1, s32[32]{0:T(128)} %refs_1_.1, s32[4,4]{1,0:T(4,128)} %refs_2_.1, s32[4]{0:T(128)} %refs_3_.1, s32[4,4]{1,0:T(4,128)} %refs_4_.1, s32[4,4]{1,0:T(4,128)} %refs_5_.1, s32[4]{0:T(128)} %refs_6_.1, s32[2,16]{1,0:T(2,128)} %refs_7_.1, s32[2,16]{1,0:T(2,128)} %refs_8_.1, ...), custom_call_target="tpu_custom_call" | custom-call | tf_op jit(solution)/shard_map/pallas_call | solution.py:674
  16.5 0.7 %copy.19 = f32[5,32,512]{2,1,0:T(8,128)} copy(f32[5,32,512]{2,1,0:T(8,128)S(1)} %shard_map.163) | data formatting | bytes 655360

commit v7 on v6

--- a/solution.py
+++ b/solution.py
@@ -232,7 +232,6 @@
         return spread_down(jnp.where(own, row, 0), cap_curve)
 
     out_keys = jnp.concatenate([tile_key_rows(p, True) for p in to_peer], axis=0)
-    in_keys = jnp.concatenate([tile_key_rows(p, False) for p in from_peer], axis=0)
     rim_keys = jnp.concatenate([curve_key_rows(side) for side in range(2)], axis=0)
 
     sub_iota = lax.broadcasted_iota(jnp.int32, (8, 128), 0)
@@ -268,26 +267,13 @@
     lane_t = lax.broadcasted_iota(jnp.int32, (tile_rows, 128), 1)
     low_t = lane_t < 64
     out_is_send = half_flags((tile_rows, 128), 0, True)
-    in_is_send = half_flags((tile_rows, 128), 0, False)
     out_elem, out_face, out_child, out_turn = decode(down_rows(out_keys), out_is_send)
-    in_elem, in_face, in_child, in_turn = decode(down_rows(in_keys), in_is_send)
     out_y = out_face < 4
-    in_y = in_face < 4
     out_code = jnp.where(out_is_send, out_child, 5 + out_turn)
-    in_code = jnp.where(in_is_send, 8 + in_child, in_turn)
     upper_t = jnp.where(low_t, 0, 1)
     out_masks = [jnp.where(out_code == 2 * j + upper_t, 1.0, 0.0) for j in range(7)]
-    extra_masks = [
-        jnp.where(jnp.logical_and(out_is_send, out_code == 2 * j + upper_t), 1.0, 0.0)
-        for j in range(2)
-    ]
     out_sign = jnp.where(out_is_send, -1.0, 1.0)
-    in_sign_half = jnp.where(in_is_send, 0.5, -0.5)
     out_match = low_t == out_y
-    in_match = low_t == in_y
-    in_low_faces = jnp.where(jnp.logical_and(in_match, jnp.logical_not(in_is_send)), 1.0, 0.0)
-    in_high_faces = jnp.where(jnp.logical_and(in_match, in_is_send), 1.0, 0.0)
-    out_high_faces = jnp.where(jnp.logical_and(out_match, out_is_send), 1.0, 0.0)
 
     rim_row = lax.broadcasted_iota(jnp.int32, (curve_rows, 128), 0)
     lane_c = lax.broadcasted_iota(jnp.int32, (curve_rows, 128), 1)
@@ -296,10 +282,6 @@
     rim_first = rim_row < cap_curve
     rim_match = low_c == rim_first
     rim_sign = jnp.where(rim_first, 1.0, -1.0)
-    upper_c = jnp.where(low_c, 0, 1)
-    in_masks = [jnp.where(in_code == 2 * j + upper_t, 1.0, 0.0) for j in range(7)]
-    rim_masks = [jnp.where(rim_turn == 2 * j + upper_c, 1.0, 0.0) for j in range(4)]
-    rim_place = jnp.where(rim_match, 1.0, 0.0)
 
     def one_hot(flags):
         return jnp.where(flags, 1.0, 0.0).astype(half_type)
@@ -309,59 +291,99 @@
     rim_lane = lax.broadcasted_iota(jnp.int32, (curve_rows, 2 * elements), 1) % elements
     rim_gather = one_hot(rim_lane == rim_elem[:, : 2 * elements])
 
-    lane_shape = (elements, 4 * tile_rows)
-    lane_s = lax.broadcasted_iota(jnp.int32, lane_shape, 1)
-    in_part = lane_s < 2 * tile_rows
-    first_half = (lane_s & (block - 1)) < half_rows
-    lane_from_send = first_half != in_part
-    t_elem, t_face, _, _ = decode(
-        jnp.where(in_part, along_lanes(in_keys, 4), along_lanes(out_keys, 4)), lane_from_send
-    )
-    t_hit = t_elem == lax.broadcasted_iota(jnp.int32, lane_shape, 0)
-    tile_scatter = one_hot(t_hit)
-    rim_shape = (elements, 2 * curve_rows)
-    c_elem, c_face, _, _ = decode(
-        along_lanes(rim_keys, 2), lax.broadcasted_iota(jnp.int32, rim_shape, 1) < 0
-    )
-    c_hit = c_elem == lax.broadcasted_iota(jnp.int32, rim_shape, 0)
-    rim_scatter = one_hot(c_hit)
-
-    def any_lane(flags):
-        return jnp.max(jnp.where(flags, 1.0, 0.0), axis=1, keepdims=True)
-
-    listed = [any_lane(jnp.logical_and(c_hit, c_face == f)) for f in (0, 1)]
-    listed += [any_lane(jnp.logical_and(t_hit, t_face == f)) for f in (2, 3, 4, 5)]
-
-    scale_blocks = []
-    for start in range(0, elements, 8):
-        value = jnp.zeros((8, 128), jnp.int32)
-        for at in range(8):
-            value = jnp.where(sub_iota == at, jnp.int32(1) << levels_ref[start + at], value)
-        scale_blocks.append(value.astype(jnp.float32))
-    scale = jnp.concatenate(scale_blocks, axis=0)
-    scale = jnp.concatenate([scale] * 4, axis=1)
-    vol_scale = scale * (-time_step)
-    lift = scale * (28.0 * time_step)
-
-    node = lax.broadcasted_iota(jnp.int32, (elements, 512), 1)
-    vel_to_sum = []
-    pres_to_vel = []
-    own_damp = []
-    side_damp = []
-    for dim in range(3):
-        place = (node >> (6 - 3 * dim)) & 7
-        low_end = place == 0
-        high_end = place == 7
-        on_face = jnp.logical_or(low_end, high_end)
-        known = jnp.where(low_end, listed[2 * dim], listed[2 * dim + 1])
-        strong = jnp.where(on_face, lift * (1.0 - 0.5 * known), 0.0)
-        weak = jnp.where(on_face, lift * (0.5 * known), 0.0)
-        vel_to_sum.append(jnp.where(low_end, -strong, strong))
-        pres_to_vel.append(jnp.where(low_end, -weak, weak))
-        own_damp.append(strong)
-        side_damp.append(weak)
-    total_damp = side_damp[0] + side_damp[1] + side_damp[2]
-    vel_damp = [own_damp[d] + (total_damp - side_damp[d]) for d in range(3)]
+    def late_tables():
+        in_keys = jnp.concatenate([tile_key_rows(p, False) for p in from_peer], axis=0)
+        in_is_send = half_flags((tile_rows, 128), 0, False)
+        in_elem, in_face, in_child, in_turn = decode(down_rows(in_keys), in_is_send)
+        in_y = in_face < 4
+        in_code = jnp.where(in_is_send, 8 + in_child, in_turn)
+        extra_masks = [
+            jnp.where(jnp.logical_and(out_is_send, out_code == 2 * j + upper_t), 1.0, 0.0)
+            for j in range(2)
+        ]
+        in_sign_half = jnp.where(in_is_send, 0.5, -0.5)
+        in_match = low_t == in_y
+        in_low_faces = jnp.where(jnp.logical_and(in_match, jnp.logical_not(in_is_send)), 1.0, 0.0)
+        in_high_faces = jnp.where(jnp.logical_and(in_match, in_is_send), 1.0, 0.0)
+        out_high_faces = jnp.where(jnp.logical_and(out_match, out_is_send), 1.0, 0.0)
+        upper_c = jnp.where(low_c, 0, 1)
+        in_masks = [jnp.where(in_code == 2 * j + upper_t, 1.0, 0.0) for j in range(7)]
+        rim_masks = [jnp.where(rim_turn == 2 * j + upper_c, 1.0, 0.0) for j in range(4)]
+        rim_place = jnp.where(rim_match, 1.0, 0.0)
+        lane_shape = (elements, 4 * tile_rows)
+        lane_s = lax.broadcasted_iota(jnp.int32, lane_shape, 1)
+        in_part = lane_s < 2 * tile_rows
+        first_half = (lane_s & (block - 1)) < half_rows
+        lane_from_send = first_half != in_part
+        t_elem, t_face, _, _ = decode(
+            jnp.where(in_part, along_lanes(in_keys, 4), along_lanes(out_keys, 4)), lane_from_send
+        )
+        t_hit = t_elem == lax.broadcasted_iota(jnp.int32, lane_shape, 0)
+        tile_scatter = one_hot(t_hit)
+        rim_shape = (elements, 2 * curve_rows)
+        c_elem, c_face, _, _ = decode(
+            along_lanes(rim_keys, 2), lax.broadcasted_iota(jnp.int32, rim_shape, 1) < 0
+        )
+        c_hit = c_elem == lax.broadcasted_iota(jnp.int32, rim_shape, 0)
+        rim_scatter = one_hot(c_hit)
+
+        def any_lane(flags):
+            return jnp.max(jnp.where(flags, 1.0, 0.0), axis=1, keepdims=True)
+
+        listed = [any_lane(jnp.logical_and(c_hit, c_face == f)) for f in (0, 1)]
+        listed += [any_lane(jnp.logical_and(t_hit, t_face == f)) for f in (2, 3, 4, 5)]
+
+        scale_blocks = []
+        for start in range(0, elements, 8):
+            value = jnp.zeros((8, 128), jnp.int32)
+            for at in range(8):
+                value = jnp.where(sub_iota == at, jnp.int32(1) << levels_ref[start + at], value)
+            scale_blocks.append(value.astype(jnp.float32))
+        scale = jnp.concatenate(scale_blocks, axis=0)
+        scale = jnp.concatenate([scale] * 4, axis=1)
+        vol_scale = scale * (-time_step)
+        lift = scale * (28.0 * time_step)
+
+        node = lax.broadcasted_iota(jnp.int32, (elements, 512), 1)
+        vel_to_sum = []
+        pres_to_vel = []
+        own_damp = []
+        side_damp = []
+        for dim in range(3):
+            place = (node >> (6 - 3 * dim)) & 7
+            low_end = place == 0
+            high_end = place == 7
+            on_face = jnp.logical_or(low_end, high_end)
+            known = jnp.where(low_end, listed[2 * dim], listed[2 * dim + 1])
+            strong = jnp.where(on_face, lift * (1.0 - 0.5 * known), 0.0)
+            weak = jnp.where(on_face, lift * (0.5 * known), 0.0)
+            vel_to_sum.append(jnp.where(low_end, -strong, strong))
+            pres_to_vel.append(jnp.where(low_end, -weak, weak))
+            own_damp.append(strong)
+            side_damp.append(weak)
+        total_damp = side_damp[0] + side_damp[1] + side_damp[2]
+        vel_damp = [own_damp[d] + (total_damp - side_damp[d]) for d in range(3)]
+        return {
+            "extra_masks": extra_masks,
+            "in_sign_half": in_sign_half,
+            "in_y": in_y,
+            "in_low_faces": in_low_faces,
+            "in_high_faces": in_high_faces,
+            "out_high_faces": out_high_faces,
+            "in_masks": in_masks,
+            "rim_masks": rim_masks,
+            "rim_place": rim_place,
+            "tile_scatter": tile_scatter,
+            "rim_scatter": rim_scatter,
+            "vol_scale": vol_scale,
+            "lift": lift,
+            "vel_to_sum": vel_to_sum,
+            "pres_to_vel": pres_to_vel,
+            "total_damp": total_damp,
+            "vel_damp": vel_damp,
+        }
+
+    late = {}
 
     def tile_copies(stage):
         return [
@@ -438,7 +460,8 @@
             )
             kept = jnp.where(out_match, side, 0.0)
             own_rows.append((kept + swap_halves(kept)).astype(half_type))
-        coded = dot(jnp.concatenate(own_rows, axis=0), send_mat_ref[...])
+        own_rows = jnp.concatenate(own_rows, axis=0)
+        coded = dot(own_rows, send_mat_ref[:, :896])
 
         def choose(source, rows_at, rows, masks, first):
             total = None
@@ -463,7 +486,10 @@
         for copy in copies:
             copy.start()
 
-        rest = [choose(coded, f * tile_rows, tile_rows, extra_masks, 7) for f in range(5)]
+        if stage == 0:
+            late.update(late_tables())
+        apart = dot(own_rows, send_mat_ref[:, 896:])
+        rest = [choose(apart, f * tile_rows, tile_rows, late["extra_masks"], 0) for f in range(5)]
         rest_n = jnp.where(out_y, rest[2], rest[3])
         rest_o = jnp.where(out_y, rest[3], rest[2])
         rest_p = 0.5 * (rest[4] + rest_n)
@@ -476,7 +502,7 @@
             jnp.where(out_y, rest_o, rest_n),
             rest_p,
         ]
-        rest_parts = [split(value * out_high_faces) for value in rest_fields]
+        rest_parts = [split(value * late["out_high_faces"]) for value in rest_fields]
 
         if stage == 0:
             loads[14].wait()
@@ -504,19 +530,19 @@
 
         vel_y, pres_y = banded(2, along_y_ref)
         vel_z, pres_z = banded(3, along_z_ref)
-        diverge = vol_scale * (grad_x[:elements] + vel_y + vel_z)
+        diverge = late["vol_scale"] * (grad_x[:elements] + vel_y + vel_z)
         to_sum = diverge
         for d in range(3):
-            to_sum = to_sum + vel_to_sum[d] * current[1 + d]
+            to_sum = to_sum + late["vel_to_sum"][d] * current[1 + d]
         pres_grads = (grad_x[elements:], pres_y, pres_z)
-        result = [to_sum - total_damp * current[0]]
+        result = [to_sum - late["total_damp"] * current[0]]
         for d in range(3):
             result.append(
-                vol_scale * pres_grads[d]
-                + pres_to_vel[d] * current[4]
-                - vel_damp[d] * current[1 + d]
+                late["vol_scale"] * pres_grads[d]
+                + late["pres_to_vel"][d] * current[4]
+                - late["vel_damp"][d] * current[1 + d]
             )
-        result.append(to_sum - total_damp * current[4])
+        result.append(to_sum - late["total_damp"] * current[4])
 
         if stage == 0:
             loads[13].wait()
@@ -551,14 +577,14 @@
         stacked = [fields[0][0], fields[0][1], fields[2][0], fields[2][1]]
         stacked += [fields[1][0], fields[1][1], fields[3][0], fields[3][1]]
         taken = dot(jnp.concatenate(stacked, axis=0), take_mat_ref[...])
-        tile_vals = [choose(taken, f * tile_rows, tile_rows, in_masks, 0) for f in range(4)]
+        tile_vals = [choose(taken, f * tile_rows, tile_rows, late["in_masks"], 0) for f in range(4)]
         rim_at = 4 * tile_rows
         rim_vals = [
-            choose(taken, rim_at + f * curve_rows, curve_rows, rim_masks, 0) for f in range(4)
+            choose(taken, rim_at + f * curve_rows, curve_rows, late["rim_masks"], 0) for f in range(4)
         ]
 
-        rim_cols = [jnp.concatenate(split(value * rim_place), axis=0) for value in rim_vals]
-        placed = dot(rim_scatter, jnp.concatenate(rim_cols, axis=1))
+        rim_cols = [jnp.concatenate(split(value * late["rim_place"]), axis=0) for value in rim_vals]
+        placed = dot(late["rim_scatter"], jnp.concatenate(rim_cols, axis=1))
         place_sum = -0.5 * placed[:, :128]
         place_vel = -0.5 * placed[:, 128:256]
         place_pres = jnp.where(low_e, place_vel, -place_vel)
@@ -576,19 +602,19 @@
         put = [
             put_sum,
             0.5 * tile_vals[2],
-            jnp.where(in_y, put_n, put_o),
-            jnp.where(in_y, put_o, put_n),
-            in_sign_half * tile_vals[1],
+            jnp.where(late["in_y"], put_n, put_o),
+            jnp.where(late["in_y"], put_o, put_n),
+            late["in_sign_half"] * tile_vals[1],
         ]
         zero_part = jnp.zeros((tile_rows, 128), half_type)
         columns = []
         for f in range(5):
-            first = split(put[f] * in_low_faces)
-            second = split(put[f] * in_high_faces)
+            first = split(put[f] * late["in_low_faces"])
+            second = split(put[f] * late["in_high_faces"])
             high, low = rest_parts[f]
             columns.append(jnp.concatenate([first[0], first[1], zero_part, zero_part], axis=0))
             columns.append(jnp.concatenate([second[0], second[1], high, low], axis=0))
-        on_faces = dot(tile_scatter, jnp.concatenate(columns, axis=1))
+        on_faces = dot(late["tile_scatter"], jnp.concatenate(columns, axis=1))
         spread = dot(
             jnp.concatenate(
                 [on_faces[:, 256 * f : 256 * f + 256].astype(half_type) for f in range(5)], axis=0
@@ -601,7 +627,7 @@
             first = nodes[:, :128] + jnp.where(low_e, rim_fields[f], 0.0)
             last = nodes[:, 384:] + jnp.where(low_e, 0.0, rim_fields[f])
             nodes = jnp.concatenate([first, nodes[:, 128:384], last], axis=1)
-            finished.append(result[f] + lift * nodes)
+            finished.append(result[f] + late["lift"] * nodes)
         return finished
 
     loads[0].wait()

time: 17.4 us -> 17.3 us (level)
  no operation moved by 1% of the time
where the time goes in v7:
time: 17.3 us; the launch traced here: 17.2 us
  Pallas kernels  16.5 us (95%)
  local copies, waits for them, and re-layouts  0.73 us (4%)
    pallas_call x1, Pallas kernels, shards(): pl.pallas_call(functools.partial(section_kernel, sizes), out_shape=pltpu....  16.5 us
    unnamed x1, local copies, waits for them, and re-layouts  0.73 us

profile of v7, /device:TPU:0, one launch (start us, length us, event | category | flops | bytes accessed | tf_op | source)
XLA Modules:
  0.0 17.2 jit_solution(5115131346595946672)
XLA Ops:
  0.0 16.5 %shard_map.163 = f32[5,32,512]{2,1,0:T(8,128)S(1)} custom-call(f32[5,32,512]{2,1,0:T(8,128)} %refs_0_.1, s32[32]{0:T(128)} %refs_1_.1, s32[4,4]{1,0:T(4,128)} %refs_2_.1, s32[4]{0:T(128)} %refs_3_.1, s32[4,4]{1,0:T(4,128)} %refs_4_.1, s32[4,4]{1,0:T(4,128)} %refs_5_.1, s32[4]{0:T(128)} %refs_6_.1, s32[2,16]{1,0:T(2,128)} %refs_7_.1, s32[2,16]{1,0:T(2,128)} %refs_8_.1, ...), custom_call_target="tpu_custom_call" | custom-call | tf_op jit(solution)/shard_map/pallas_call | solution.py:700
  16.5 0.7 %copy.19 = f32[5,32,512]{2,1,0:T(8,128)} copy(f32[5,32,512]{2,1,0:T(8,128)S(1)} %shard_map.163) | data formatting | bytes 655360
